TPU v7x, 32 devices: a whole 2x2x4 slice. The times are simulated.
32 devices in a mesh: freq: 4 (over z), src: 8 (over y, x, core).
Axes of the slice: x: 2, y: 2, z: 4, core: 2. Of those that a mesh axis runs over, the one named last changes fastest.
Arguments:
- reflection: bfloat16 [2, 64, 1024, 1024], P(None, 'freq', None, 'src'), may hold values from -0.1875 to 0.1875
- direct_wave: float32 [1024, 64, 128], P('src', 'freq'), may hold values from -6 to 6
- first_arrival: int32 [1024, 64], P(('src', 'freq')), may hold values from 64 to 191
Outputs:
- focus_minus: float32 [1024, 64, 128], P('src', 'freq')
- focus_plus: float32 [1024, 64, 128], P('src', 'freq')
All inputs are finite; a program needn't handle non-finite values.
Results may differ from a plain program's by a relative error of at most 0.035.
Values may be sent and summed in bfloat16 or wider, within the bound.
No kernel may reach another device: no remote copies, remote signals or barrier semaphores. Data moves between devices by JAX's collectives and lax.ppermute only.
A program may use at most 128 MiB of HBM per device.

v0:
```python
import functools
import math

import jax
import jax.numpy as jnp
import ml_dtypes
import numpy as np
from jax import lax
from jax.experimental import pallas as pl
from jax.experimental.pallas import tpu as pltpu
from jax.sharding import PartitionSpec as P

NT = 512
ITERS = 2
KEPT = 192
CHUNKS = 2
MIB = 1 << 20
WEIGHT = 3e9
UNROLL = 8
BYTES = MIB
TILE = 16
PAD = 4
TERMS_MIB = 32
OTHER_MIB = 12
BF16, F32 = jnp.bfloat16, jnp.float32


def window_tables(nfreq, chunks, groups):
    freqs = np.arange(1, nfreq + 1)
    times = np.arange(KEPT)
    phase = ((freqs[:, None] * times[None, :]) % NT).astype(np.float32) * np.float32(2.0 * math.pi / NT)
    parts = np.stack([np.cos(phase), -np.sin(phase)])
    inverse = (parts * np.float32(2.0 / NT)).astype(ml_dtypes.bfloat16)
    forward = parts.astype(ml_dtypes.bfloat16).astype(np.float32) * np.where(times == 0, 1.0, 2.0)
    forward = forward.astype(ml_dtypes.bfloat16)

    def rows(table):
        table = table.reshape(2, groups, chunks, nfreq // groups // chunks, KEPT)
        return table.transpose(0, 2, 1, 3, 4).reshape(2 * nfreq, KEPT)

    return np.ascontiguousarray(rows(inverse).T), rows(forward)


def lane_index(shape):
    return lax.broadcasted_iota(jnp.int32, shape, len(shape) - 1)


def to_chunks(by_sub, lanes):
    n = len(by_sub)
    if n == 1:
        return by_sub
    width = 64 // n
    place = (lanes % 64) // width
    result = []
    for other in range(n):
        total = None
        for a in range(n):
            shift = ((a - other) * width) % 128
            moved = pltpu.roll(by_sub[a], shift, 1) if shift else by_sub[a]
            total = moved if total is None else jnp.where(place == a, moved, total)
        result.append(total)
    return result


def pack_kernel(chunks, f_dev, rows, dw_ref, *out_refs):
    fp = f_dev // chunks
    lanes = lane_index((rows, 128))

    @pl.loop(0, fp)
    def _(b):
        values = [dw_ref[pl.ds(a * fp + b, rows, stride=f_dev), :] for a in range(chunks)]
        for out_ref, value in zip(out_refs, to_chunks(values, lanes)):
            out_ref[b] = value.astype(BF16)


def limits_kernel(chunks, arrival_ref, *refs):
    width = 64 // chunks
    for chunk, out_ref in enumerate(refs[-chunks:]):
        limit = arrival_ref[:, chunk * width : (chunk + 1) * width]
        out_ref[...] = jnp.concatenate([limit] * (2 * chunks), axis=1)


def wave_kernel(chunks, f_dev, rows, dw_ref, *refs):
    fp = f_dev // chunks
    lanes = lane_index((rows, 128))

    @pl.loop(0, fp)
    def _(b):
        values = [dw_ref[pl.ds(a * fp + b, rows, stride=f_dev), :] for a in range(chunks)]
        for out_ref, value in zip(refs[-chunks:], to_chunks(values, lanes)):
            out_ref[b] = value


def unpack_kernel(chunks, f_dev, rows, has_wave, *refs):
    fp = f_dev // chunks
    lanes = lane_index((rows, 128))
    v_refs, out_ref = refs[:chunks], refs[-1]
    for b in range(fp):
        values = [v_refs[chunk][b].astype(F32) for chunk in range(chunks)]
        for a, value in enumerate(to_chunks(values, lanes)):
            place = pl.ds(a * fp + b, rows, stride=f_dev)
            if has_wave:
                value = value + refs[chunks][place, :]
            out_ref[place, :] = value


def assemble_kernel(n_f, has_wave, where_ref, *refs):
    blocks, out_ref = refs[:n_f], refs[-1]
    rows = blocks[0].shape[1]
    for k in range(n_f):
        place = pl.ds(pl.multiple_of((where_ref[0] ^ k) * rows, rows), rows)
        value = blocks[k][...]
        if has_wave:
            value = (refs[n_f][:, place, :] + value.astype(F32)).astype(BF16)
        out_ref[:, place, :] = value


def terms_kernel(chunks, sign, places_ref, whole_ref, v_ref, *refs):
    out_ref = refs[-1]
    lanes = lane_index(v_ref.shape[1:])
    place = (lanes % 64) // (64 // chunks)

    def frequency(b):
        value = v_ref[b].astype(F32)
        turned = pltpu.roll(value, 64, 1)
        turned = jnp.where((lanes < 64) == (sign > 0), -turned, turned)
        weights = [jnp.where(place == a, x, 0.0) for a in range(chunks) for x in (value, turned)]
        weights = jnp.concatenate(weights, axis=0).astype(BF16)
        left = []
        for pos in range(out_ref.shape[0]):
            at = places_ref[pos]
            left.append(jnp.concatenate([whole_ref[p, a, b, at] for a in range(chunks) for p in range(2)], axis=1))
        total = jnp.dot(jnp.concatenate(left, axis=0), weights, preferred_element_type=F32).astype(BF16)
        rows = out_ref.shape[2]
        for pos in range(out_ref.shape[0]):
            out_ref[pos, b] = total[pos * rows : (pos + 1) * rows]

    @pl.loop(0, v_ref.shape[0] // UNROLL)
    def _(i):
        for j in range(UNROLL):
            frequency(i * UNROLL + j)


def add_kernel(n_in, *refs):
    out_ref = refs[-1]
    half = out_ref.shape[0]
    total = refs[0][half : 2 * half].astype(F32)
    for ref in refs[1:n_in]:
        total = total + ref[half : 2 * half].astype(F32)
    out_ref[...] = total.astype(BF16)


def split_kernel(n_in, n_f, where_ref, *refs):
    outs = refs[-n_f:]
    rows = outs[0].shape[1]
    for k in range(n_f):
        place = pl.ds(pl.multiple_of((where_ref[0] ^ k) * rows, rows), rows)
        total = refs[0][0, :, place, :].astype(F32)
        for ref in refs[1:n_in]:
            total = total + ref[0, :, place, :].astype(F32)
        outs[k][...] = total.astype(BF16)


def window_kernel(chunks, n_f, tile, where_ref, limit_ref, inv_ref, fwd_ref, *refs):
    blocks, outs, (gather, scatter) = refs[:n_f], refs[-n_f - 2 : -2], refs[-2:]
    fp, rows, _ = blocks[0].shape
    depth = n_f * fp
    step = depth + PAD
    for k in range(n_f):
        base = (where_ref[0] ^ k) * fp
        for b in range(fp):
            gather[pl.ds(base + b, rows, stride=step), :] = blocks[k][b].astype(F32)
    lanes = lane_index((depth, 128))
    part, place = lanes // 64, (lanes % 64) // (64 // chunks)
    times = lax.broadcasted_iota(jnp.int32, (KEPT, 128), 0)
    width = 64 // chunks
    for first in range(0, rows, tile):
        columns = []
        for r in range(first, first + tile):
            value = gather[pl.ds(r * step, depth), :]
            spread = []
            for a in range(chunks):
                total = value
                for other in range(chunks):
                    if other != a:
                        total = jnp.where(place == other, pltpu.roll(value, ((other - a) * width) % 128, 1), total)
                spread.append(total)
            stacked = [jnp.where(part == p, x, 0.0) for p in range(2) for x in spread]
            columns.append(jnp.concatenate(stacked, axis=0).astype(BF16))
        signal = jnp.dot(inv_ref[...], jnp.concatenate(columns, axis=1), preferred_element_type=F32)
        kept = []
        for i in range(tile):
            limit = limit_ref[pl.ds(first + i, 1), :]
            kept.append(jnp.where(times < limit, signal[:, i * 128 : (i + 1) * 128], 0.0).astype(BF16))
        back = jnp.dot(fwd_ref[...], jnp.concatenate(kept, axis=1), preferred_element_type=F32)
        for i in range(tile):
            total = None
            for p in range(2):
                for a in range(chunks):
                    at = (p * chunks + a) * depth
                    piece = back[at : at + depth, i * 128 : (i + 1) * 128]
                    total = piece if total is None else jnp.where((part == p) & (place == a), piece, total)
            scatter[pl.ds((first + i) * step, depth), :] = total
    for k in range(n_f):
        base = (where_ref[0] ^ k) * fp
        for b in range(fp):
            outs[k][b] = scatter[pl.ds(base + b, rows, stride=step), :].astype(BF16)


def vmem():
    return pl.BlockSpec(memory_space=pltpu.VMEM)


def anywhere():
    return pl.BlockSpec(memory_space=pl.ANY)


def smem():
    return pl.BlockSpec(memory_space=pltpu.SMEM)


def params(mib):
    return pltpu.CompilerParams(vmem_limit_bytes=mib * MIB)


def cost(flops, nbytes):
    return pl.CostEstimate(flops=int(flops), bytes_accessed=int(nbytes), transcendentals=0)


def bf16(*shape):
    return jax.ShapeDtypeStruct(shape, BF16)


class Plan:
    def __init__(self, reflection, direct_wave):
        self.n_f, self.n_s = lax.axis_size("freq"), lax.axis_size("src")
        self.q, self.f_dev, _ = direct_wave.shape
        self.chunks = CHUNKS
        self.fp = self.f_dev // self.chunks
        self.own_rows = self.q // self.n_f
        self.n_chip = self.n_s // 2
        self.bits = self.n_chip.bit_length() - 1
        z, s = lax.axis_index("freq"), lax.axis_index("src")
        chip, self.core = s // 2, s % 2
        self.where = z.reshape(1).astype(jnp.int32)
        orders = np.zeros((2, self.n_chip), np.int32)
        for core in range(2):
            for pos in range(self.n_chip):
                for stage in range(self.bits):
                    if pos >> (self.bits - 1 - stage) & 1:
                        orders[core, pos] ^= self.mask(stage, core)
        orders = jnp.asarray(orders)
        self.near = ((chip ^ orders[self.core]) * 2 + self.core).astype(jnp.int32)
        self.far = ((chip ^ orders[1 - self.core]) * 2 + 1 - self.core).astype(jnp.int32)
        inverse, forward = window_tables(self.n_f * self.f_dev, self.chunks, self.n_f)
        self.tables = [jnp.asarray(inverse), jnp.asarray(forward)]
        self.reflection = reflection.reshape(2, self.chunks, self.fp, self.n_s, self.q, self.q)

    def mask(self, stage, core):
        return 1 << ((stage + core) % self.bits)

    def to_core(self, value):
        return lax.ppermute(value, "src", [(s, s ^ 1) for s in range(self.n_s)])

    def to_chip(self, value, stage):
        pairs = [(s, s ^ (self.mask(stage, s % 2) << 1)) for s in range(self.n_s)]
        return lax.ppermute(value, "src", pairs)

    def to_group(self, value, k):
        return lax.ppermute(value, "freq", [(z, z ^ k) for z in range(self.n_f)])

    def exchange(self, blocks):
        moved = {k: self.to_group(blocks[k], k) for k in range(self.n_f - 1, 0, -1)}
        return [blocks[0]] + [moved[k] for k in range(1, self.n_f)]

    def pack(self, direct_wave):
        return pl.pallas_call(
            functools.partial(pack_kernel, self.chunks, self.f_dev, self.q),
            out_shape=[bf16(self.fp, self.q, 128)] * self.chunks,
            in_specs=[vmem()],
            out_specs=[vmem()] * self.chunks,
            compiler_params=params(OTHER_MIB),
            cost_estimate=cost(WEIGHT, BYTES),
            name="pack",
        )(direct_wave.reshape(self.q * self.f_dev, 128))

    def make_limits(self, first_arrival, after):
        self.limits = pl.pallas_call(
            functools.partial(limits_kernel, self.chunks),
            out_shape=[jax.ShapeDtypeStruct((self.own_rows, 128), jnp.int32)] * self.chunks,
            in_specs=[vmem()] + [anywhere()] * len(after),
            out_specs=[vmem()] * self.chunks,
            compiler_params=params(OTHER_MIB),
            cost_estimate=cost(WEIGHT, BYTES),
            name="limits",
        )(first_arrival, *after)
        return self.limits[:1]

    def waves(self, direct_wave, after):
        n = self.chunks
        return pl.pallas_call(
            functools.partial(wave_kernel, n, self.f_dev, self.q),
            out_shape=[jax.ShapeDtypeStruct((self.fp, self.q, 128), F32)] * n,
            in_specs=[vmem()] + [anywhere()] * len(after),
            out_specs=[vmem()] * n,
            compiler_params=params(OTHER_MIB),
            name="wave",
        )(direct_wave.reshape(self.q * self.f_dev, 128), *after)

    def unpack(self, values, wave=None):
        waves = [] if wave is None else [wave.reshape(self.q * self.f_dev, 128)]
        out = pl.pallas_call(
            functools.partial(unpack_kernel, self.chunks, self.f_dev, self.q, wave is not None),
            out_shape=jax.ShapeDtypeStruct((self.q * self.f_dev, 128), F32),
            in_specs=[vmem()] * (self.chunks + len(waves)),
            out_specs=vmem(),
            compiler_params=params(OTHER_MIB),
            name="unpack",
        )(*values, *waves)
        return out.reshape(self.q, self.f_dev, 128)

    def assemble(self, blocks, wave, after):
        waves = [] if wave is None else [wave]
        return pl.pallas_call(
            functools.partial(assemble_kernel, self.n_f, wave is not None),
            out_shape=bf16(self.fp, self.q, 128),
            in_specs=[smem()] + [vmem()] * (self.n_f + len(waves)) + [anywhere()] * len(after),
            out_specs=vmem(),
            compiler_params=params(OTHER_MIB),
            cost_estimate=cost(WEIGHT, BYTES),
            name="assemble",
        )(self.where, *blocks, *waves, *after)

    def terms(self, vector, places, sign, after):
        return pl.pallas_call(
            functools.partial(terms_kernel, self.chunks, sign),
            out_shape=bf16(self.n_chip, self.fp, self.q, 128),
            in_specs=[smem()] + [vmem()] * 2 + [anywhere()] * len(after),
            out_specs=vmem(),
            compiler_params=params(TERMS_MIB),
            cost_estimate=cost(WEIGHT, BYTES),
            name="terms",
        )(places, self.reflection, vector, *after)

    def add(self, values, half, after):
        return pl.pallas_call(
            functools.partial(add_kernel, len(values)),
            out_shape=bf16(half, self.fp, self.q, 128),
            in_specs=[vmem()] * len(values) + [anywhere()] * len(after),
            out_specs=vmem(),
            compiler_params=params(OTHER_MIB),
            cost_estimate=cost(WEIGHT, BYTES),
            name="add",
        )(*values, *after)

    def split(self, values, after):
        out = bf16(self.fp, self.own_rows, 128)
        return pl.pallas_call(
            functools.partial(split_kernel, len(values), self.n_f),
            out_shape=[out] * self.n_f,
            in_specs=[smem()] + [vmem()] * len(values) + [anywhere()] * len(after),
            out_specs=[vmem()] * self.n_f,
            compiler_params=params(OTHER_MIB),
            cost_estimate=cost(WEIGHT, BYTES),
            name="split",
        )(self.where, *values, *after)

    def window(self, blocks, chunk, after):
        out = bf16(self.fp, self.own_rows, 128)
        depth = self.n_f * self.fp + PAD
        scratch = pltpu.VMEM((self.own_rows * depth, 128), F32)
        return pl.pallas_call(
            functools.partial(window_kernel, self.chunks, self.n_f, min(TILE, self.own_rows)),
            out_shape=[out] * self.n_f,
            in_specs=[smem()] + [vmem()] * (3 + self.n_f) + [anywhere()] * len(after),
            out_specs=[vmem()] * self.n_f,
            scratch_shapes=[scratch, scratch],
            compiler_params=params(OTHER_MIB),
            cost_estimate=cost(WEIGHT, BYTES),
            name="window",
        )(self.where, self.limits[chunk], *self.tables, *blocks, *after)


class Chain:
    def __init__(self, plan, chunk, vector):
        self.plan, self.chunk, self.wave = plan, chunk, None
        self.vector, self.done, self.minus = vector, 0, None
        self.todo = self.theta()

    def theta(self):
        return [self.far, self.near] + [self.add] * self.plan.bits + [self.split, self.window, self.assemble]

    def step(self, after):
        return self.todo.pop(0)(after)

    def sign(self):
        return 1 if self.done % 2 == 0 else -1

    def far(self, after):
        out = self.plan.terms(self.vector, self.plan.far, self.sign(), after)
        self.arriving = self.plan.to_core(out)
        return [out]

    def near(self, after):
        out = self.plan.terms(self.vector, self.plan.near, self.sign(), after)
        self.addends, self.half = [out, self.arriving], self.plan.n_chip
        return [out]

    def add(self, after):
        plan = self.plan
        self.half //= 2
        send = plan.add(self.addends, self.half, after)
        self.addends.append(plan.to_chip(send, len(self.addends) - 2))
        return [send]

    def split(self, after):
        blocks = self.plan.split(self.addends, after)
        self.blocks = self.plan.exchange(blocks)
        return [blocks[0]]

    def window(self, after):
        blocks = self.plan.window(self.blocks, self.chunk, after)
        self.blocks = self.plan.exchange(blocks)
        return [blocks[0]]

    def assemble(self, after):
        self.done += 1
        wave = self.wave if self.done % 2 == 0 and self.done < 2 * ITERS else None
        self.vector = self.plan.assemble(self.blocks, wave, after)
        if self.done == 2 * ITERS - 1:
            self.minus = self.vector
        self.todo = self.theta()
        return [self.vector]


def local(reflection, direct_wave, first_arrival):
    plan = Plan(reflection, direct_wave)
    plus = plan.pack(direct_wave)
    chains = [Chain(plan, i, plus[i]) for i in range(plan.chunks)]
    first, second = chains[0], chains[-1]
    after = []
    for step in range(2 * ITERS):
        for place, chain in enumerate([first, first, second, first, second, second]):
            if step and place in (0, 2):
                after = chain.step(after)
            after = chain.step(after)
        if step == 0:
            after = plan.make_limits(first_arrival, after)
        if step == 1:
            waves = plan.waves(direct_wave, after)
            after = waves[:1]
            for chain, wave in zip(chains, waves):
                chain.wave = wave
        for _ in range(1 + plan.bits):
            for chain in chains:
                after = chain.step(after)
    for chain in chains:
        after = chain.step(after)
    return plan.unpack([c.minus for c in chains]), plan.unpack([c.vector for c in chains], direct_wave)


def solution(mesh):
    in_specs = (P(None, "freq", None, "src"), P("src", "freq", None), P(("src", "freq"), None))
    out_specs = (P("src", "freq", None), P("src", "freq", None))
    return jax.shard_map(local, mesh=mesh, in_specs=in_specs, out_specs=out_specs, check_vma=False)
```

profile of v0, /device:TPU:0, one launch (start us, length us, event | category | flops | bytes accessed | tf_op | source)
XLA Modules:
  0.0 214.4 jit_solution(13931072487993038614)
XLA Ops:
  3.0 3.4 %copy-done.2 = bf16[2,16,1024,128]{3,2,1,0:T(8,128)(2,1)S(1)} copy-done((bf16[2,16,1024,128]{3,2,1,0:T(8,128)(2,1)S(1)}, bf16[2,16,1024,128]{3,2,1,0:T(8,128)(2,1)}, u32[]{:S(2)}) %copy-start.2) | copy-done | bytes 8388632
  6.3 2.8 %terms.16.refs_0_ = bf16[4,8,128,128]{3,2,1,0:T(8,128)(2,1)} custom-call(s32[4]{0:T(128)S(1)} %get-tuple-element.142.places_ref, bf16[2,2,8,8,128,128]{5,4,3,2,1,0:T(8,128)(2,1)S(1)} %bitcast.12, bf16[8,128,128]{2,1,0:T(8,128)(2,1)S(1)} %get-tuple-element.73.v_ref), custom_call_target="tpu_custom_call" | custom-call | flops 3000000000 | bytes 1048576 | tf_op jit(solution)/shard_map/terms/pallas_call | solution.py:335
  11.5 1.9 terms.18.refs_2_
  15.8 3.0 %collective-permute-start.2 = (bf16[2,8,128,128]{3,2,1,0:T(8,128)(2,1)S(1)}, bf16[2,8,128,128]{3,2,1,0:T(8,128)(2,1)S(1)}, u32[]{:S(2)}, u32[]{:S(2)}) collective-permute-start(bf16[2,8,128,128]{3,2,1,0:T(8,128)(2,1)S(1)} %add.51.refs_0_), channel_id=1, source_target_pairs={{0,2},{1,5},{2,0},{3,7},{4,6},{5,1},{6,4},{7,3},{8,10},{9,13},{10,... | collective-permute-start | bytes 1572872 | tf_op jit(solution)/shard_map/ppermute | solution.py:267
  18.8 3.4 %copy-done.3 = bf16[2,16,1024,128]{3,2,1,0:T(8,128)(2,1)S(1)} copy-done((bf16[2,16,1024,128]{3,2,1,0:T(8,128)(2,1)S(1)}, bf16[2,16,1024,128]{3,2,1,0:T(8,128)(2,1)}, u32[]{:S(2)}) %copy-start.3) | copy-done | bytes 8388632
  26.0 2.1 collective-permute-start.3
  28.1 8.1 %collective-permute-done.4.refs_2_ = bf16[2,8,128,128]{3,2,1,0:T(8,128)(2,1)S(1)} collective-permute-done((bf16[2,8,128,128]{3,2,1,0:T(8,128)(2,1)S(1)}, bf16[2,8,128,128]{3,2,1,0:T(8,128)(2,1)S(1)}, u32[]{:S(2)}, u32[]{:S(2)}) %collective-permute-start.4) | collective-permute-done | bytes 524320 | tf_op jit(solution)/shard_map/ppermute | solution.py:267
  36.3 2.2 %collective-permute-start.8 = (bf16[1,8,128,128]{3,2,1,0:T(8,128)(2,1)S(1)}, bf16[1,8,128,128]{3,2,1,0:T(8,128)(2,1)S(1)}, u32[]{:S(2)}, u32[]{:S(2)}) collective-permute-start(bf16[1,8,128,128]{3,2,1,0:T(8,128)(2,1)S(1)} %add.54.refs_4_), channel_id=1, source_target_pairs={{0,4},{1,3},{2,6},{3,1},{4,0},{5,7},{6,2},{7,5},{8,12},{9,11},{10,... | collective-permute-start | bytes 786440 | tf_op jit(solution)/shard_map/ppermute | solution.py:267
  38.7 2.1 %collective-permute-start.5 = (bf16[8,32,128]{2,1,0:T(8,128)(2,1)S(1)}, bf16[8,32,128]{2,1,0:T(8,128)(2,1)S(1)}, u32[]{:S(2)}, u32[]{:S(2)}) collective-permute-start(bf16[8,32,128]{2,1,0:T(8,128)(2,1)S(1)} %get-tuple-element.76), channel_id=1, source_target_pairs={{0,8},{8,0},{16,24},{24,16},{1,9},{9,1},{17,25},{25,17},{2,10},{10... | collective-permute-start | bytes 196616 | tf_op jit(solution)/shard_map/ppermute | solution.py:270
  40.8 2.6 %collective-permute-start.6 = (bf16[8,32,128]{2,1,0:T(8,128)(2,1)S(1)}, bf16[8,32,128]{2,1,0:T(8,128)(2,1)S(1)}, u32[]{:S(2)}, u32[]{:S(2)}) collective-permute-start(bf16[8,32,128]{2,1,0:T(8,128)(2,1)S(1)} %get-tuple-element.77), channel_id=1, source_target_pairs={{0,16},{8,24},{16,0},{24,8},{1,17},{9,25},{17,1},{25,9},{2,18},{10... | collective-permute-start | bytes 196616 | tf_op jit(solution)/shard_map/ppermute | solution.py:270
  45.1 2.8 %collective-permute-start.13 = (bf16[8,32,128]{2,1,0:T(8,128)(2,1)S(1)}, bf16[8,32,128]{2,1,0:T(8,128)(2,1)S(1)}, u32[]{:S(2)}, u32[]{:S(2)}) collective-permute-start(bf16[8,32,128]{2,1,0:T(8,128)(2,1)S(1)} %get-tuple-element.86), channel_id=1, source_target_pairs={{0,16},{8,24},{16,0},{24,8},{1,17},{9,25},{17,1},{25,9},{2,18},{10... | collective-permute-start | bytes 196616 | tf_op jit(solution)/shard_map/ppermute | solution.py:270
  51.0 3.3 %collective-permute-start.9 = (bf16[8,32,128]{2,1,0:T(8,128)(2,1)S(1)}, bf16[8,32,128]{2,1,0:T(8,128)(2,1)S(1)}, u32[]{:S(2)}, u32[]{:S(2)}) collective-permute-start(bf16[8,32,128]{2,1,0:T(8,128)(2,1)S(1)} %get-tuple-element.81), channel_id=1, source_target_pairs={{0,8},{8,0},{16,24},{24,16},{1,9},{9,1},{17,25},{25,17},{2,10},{10... | collective-permute-start | bytes 196616 | tf_op jit(solution)/shard_map/ppermute | solution.py:270
  54.3 2.1 collective-permute-start.10
  59.6 2.4 %collective-permute-start.17 = (bf16[8,32,128]{2,1,0:T(8,128)(2,1)S(1)}, bf16[8,32,128]{2,1,0:T(8,128)(2,1)S(1)}, u32[]{:S(2)}, u32[]{:S(2)}) collective-permute-start(bf16[8,32,128]{2,1,0:T(8,128)(2,1)S(1)} %get-tuple-element.90), channel_id=1, source_target_pairs={{0,16},{8,24},{16,0},{24,8},{1,17},{9,25},{17,1},{25,9},{2,18},{10... | collective-permute-start | bytes 196616 | tf_op jit(solution)/shard_map/ppermute | solution.py:270
  75.5 4.1 %collective-permute-done.19.refs_2_ = bf16[2,8,128,128]{3,2,1,0:T(8,128)(2,1)S(1)} collective-permute-done((bf16[2,8,128,128]{3,2,1,0:T(8,128)(2,1)S(1)}, bf16[2,8,128,128]{3,2,1,0:T(8,128)(2,1)S(1)}, u32[]{:S(2)}, u32[]{:S(2)}) %collective-permute-start.19) | collective-permute-done | bytes 524320 | tf_op jit(solution)/shard_map/ppermute | solution.py:267
  80.4 7.7 %collective-permute-done.22.refs_2_ = bf16[2,8,128,128]{3,2,1,0:T(8,128)(2,1)S(1)} collective-permute-done((bf16[2,8,128,128]{3,2,1,0:T(8,128)(2,1)S(1)}, bf16[2,8,128,128]{3,2,1,0:T(8,128)(2,1)S(1)}, u32[]{:S(2)}, u32[]{:S(2)}) %collective-permute-start.22) | collective-permute-done | bytes 524320 | tf_op jit(solution)/shard_map/ppermute | solution.py:267
  94.8 2.7 %collective-permute-start.31 = (bf16[8,32,128]{2,1,0:T(8,128)(2,1)S(1)}, bf16[8,32,128]{2,1,0:T(8,128)(2,1)S(1)}, u32[]{:S(2)}, u32[]{:S(2)}) collective-permute-start(bf16[8,32,128]{2,1,0:T(8,128)(2,1)S(1)} %get-tuple-element.103), channel_id=1, source_target_pairs={{0,16},{8,24},{16,0},{24,8},{1,17},{9,25},{17,1},{25,9},{2,18},{10... | collective-permute-start | bytes 196616 | tf_op jit(solution)/shard_map/ppermute | solution.py:270
  112.4 1.9 terms.25.refs_5_.refs_0_
  121.2 5.1 %collective-permute-done.37.refs_2_ = bf16[2,8,128,128]{3,2,1,0:T(8,128)(2,1)S(1)} collective-permute-done((bf16[2,8,128,128]{3,2,1,0:T(8,128)(2,1)S(1)}, bf16[2,8,128,128]{3,2,1,0:T(8,128)(2,1)S(1)}, u32[]{:S(2)}, u32[]{:S(2)}) %collective-permute-start.37) | collective-permute-done | bytes 524320 | tf_op jit(solution)/shard_map/ppermute | solution.py:267
  127.2 7.6 %collective-permute-done.40.refs_2_ = bf16[2,8,128,128]{3,2,1,0:T(8,128)(2,1)S(1)} collective-permute-done((bf16[2,8,128,128]{3,2,1,0:T(8,128)(2,1)S(1)}, bf16[2,8,128,128]{3,2,1,0:T(8,128)(2,1)S(1)}, u32[]{:S(2)}, u32[]{:S(2)}) %collective-permute-start.40) | collective-permute-done | bytes 524320 | tf_op jit(solution)/shard_map/ppermute | solution.py:267
  138.1 2.0 collective-permute-start.43
  141.4 1.9 collective-permute-start.48
  147.3 2.0 collective-permute-start.45
  153.3 2.5 %collective-permute-start.51 = (bf16[8,32,128]{2,1,0:T(8,128)(2,1)S(1)}, bf16[8,32,128]{2,1,0:T(8,128)(2,1)S(1)}, u32[]{:S(2)}, u32[]{:S(2)}) collective-permute-start(bf16[8,32,128]{2,1,0:T(8,128)(2,1)S(1)} %get-tuple-element.123), channel_id=1, source_target_pairs={{0,8},{8,0},{16,24},{24,16},{1,9},{9,1},{17,25},{25,17},{2,10},{10... | collective-permute-start | bytes 196616 | tf_op jit(solution)/shard_map/ppermute | solution.py:270
  155.8 3.0 %collective-permute-start.52 = (bf16[8,32,128]{2,1,0:T(8,128)(2,1)S(1)}, bf16[8,32,128]{2,1,0:T(8,128)(2,1)S(1)}, u32[]{:S(2)}, u32[]{:S(2)}) collective-permute-start(bf16[8,32,128]{2,1,0:T(8,128)(2,1)S(1)} %get-tuple-element.124), channel_id=1, source_target_pairs={{0,16},{8,24},{16,0},{24,8},{1,17},{9,25},{17,1},{25,9},{2,18},{10... | collective-permute-start | bytes 196616 | tf_op jit(solution)/shard_map/ppermute | solution.py:270
  172.8 3.5 %collective-permute-done.55.refs_2_ = bf16[2,8,128,128]{3,2,1,0:T(8,128)(2,1)S(1)} collective-permute-done((bf16[2,8,128,128]{3,2,1,0:T(8,128)(2,1)S(1)}, bf16[2,8,128,128]{3,2,1,0:T(8,128)(2,1)S(1)}, u32[]{:S(2)}, u32[]{:S(2)}) %collective-permute-start.55) | collective-permute-done | bytes 524320 | tf_op jit(solution)/shard_map/ppermute | solution.py:267
  177.7 7.0 %collective-permute-done.58.refs_2_ = bf16[2,8,128,128]{3,2,1,0:T(8,128)(2,1)S(1)} collective-permute-done((bf16[2,8,128,128]{3,2,1,0:T(8,128)(2,1)S(1)}, bf16[2,8,128,128]{3,2,1,0:T(8,128)(2,1)S(1)}, u32[]{:S(2)}, u32[]{:S(2)}) %collective-permute-start.58) | collective-permute-done | bytes 524320 | tf_op jit(solution)/shard_map/ppermute | solution.py:267
  192.1 2.1 collective-permute-start.67
  197.6 3.3 %collective-permute-start.63 = (bf16[8,32,128]{2,1,0:T(8,128)(2,1)S(1)}, bf16[8,32,128]{2,1,0:T(8,128)(2,1)S(1)}, u32[]{:S(2)}, u32[]{:S(2)}) collective-permute-start(bf16[8,32,128]{2,1,0:T(8,128)(2,1)S(1)} %get-tuple-element.132), channel_id=1, source_target_pairs={{0,8},{8,0},{16,24},{24,16},{1,9},{9,1},{17,25},{25,17},{2,10},{10... | collective-permute-start | bytes 196616 | tf_op jit(solution)/shard_map/ppermute | solution.py:270
  200.9 2.4 %collective-permute-start.65 = (bf16[8,32,128]{2,1,0:T(8,128)(2,1)S(1)}, bf16[8,32,128]{2,1,0:T(8,128)(2,1)S(1)}, u32[]{:S(2)}, u32[]{:S(2)}) collective-permute-start(bf16[8,32,128]{2,1,0:T(8,128)(2,1)S(1)} %get-tuple-element.134), channel_id=1, source_target_pairs={{0,24},{8,16},{16,8},{24,0},{1,25},{9,17},{17,9},{25,1},{2,26},{10... | collective-permute-start | bytes 196616 | tf_op jit(solution)/shard_map/ppermute | solution.py:270
  206.5 2.4 %collective-permute-start.71 = (bf16[8,32,128]{2,1,0:T(8,128)(2,1)S(1)}, bf16[8,32,128]{2,1,0:T(8,128)(2,1)S(1)}, u32[]{:S(2)}, u32[]{:S(2)}) collective-permute-start(bf16[8,32,128]{2,1,0:T(8,128)(2,1)S(1)} %get-tuple-element.141), channel_id=1, source_target_pairs={{0,24},{8,16},{16,8},{24,0},{1,25},{9,17},{17,9},{25,1},{2,26},{10... | collective-permute-start | bytes 196616 | tf_op jit(solution)/shard_map/ppermute | solution.py:270
  209.0 2.5 %collective-permute-done.70.refs_2_ = bf16[8,32,128]{2,1,0:T(8,128)(2,1)S(1)} collective-permute-done((bf16[8,32,128]{2,1,0:T(8,128)(2,1)S(1)}, bf16[8,32,128]{2,1,0:T(8,128)(2,1)S(1)}, u32[]{:S(2)}, u32[]{:S(2)}) %collective-permute-start.70) | collective-permute-done | bytes 65568 | tf_op jit(solution)/shard_map/ppermute | solution.py:270
  (199 shorter events, 107.1 us)
Async XLA Ops:
  14.3 9.7 %collective-permute-start.1 = (bf16[4,8,128,128]{3,2,1,0:T(8,128)(2,1)S(1)}, bf16[4,8,128,128]{3,2,1,0:T(8,128)(2,1)S(1)}, u32[]{:S(2)}, u32[]{:S(2)}) collective-permute-start(bf16[4,8,128,128]{3,2,1,0:T(8,128)(2,1)S(1)} %terms.18.refs_2_), channel_id=1, source_target_pairs={{0,1},{1,0},{2,3},{3,2},{4,5},{5,4},{6,7},{7,6},{8,9},{9,8},{10,11... | collective-permute-start | bytes 3145736 | tf_op jit(solution)/shard_map/ppermute | solution.py:263
  15.8 10.2 %collective-permute-start.2 = (bf16[2,8,128,128]{3,2,1,0:T(8,128)(2,1)S(1)}, bf16[2,8,128,128]{3,2,1,0:T(8,128)(2,1)S(1)}, u32[]{:S(2)}, u32[]{:S(2)}) collective-permute-start(bf16[2,8,128,128]{3,2,1,0:T(8,128)(2,1)S(1)} %add.51.refs_0_), channel_id=1, source_target_pairs={{0,2},{1,5},{2,0},{3,7},{4,6},{5,1},{6,4},{7,3},{8,10},{9,13},{10,... | collective-permute-start | bytes 1572872 | tf_op jit(solution)/shard_map/ppermute | solution.py:267
  24.1 12.1 %collective-permute-start.4 = (bf16[2,8,128,128]{3,2,1,0:T(8,128)(2,1)S(1)}, bf16[2,8,128,128]{3,2,1,0:T(8,128)(2,1)S(1)}, u32[]{:S(2)}, u32[]{:S(2)}) collective-permute-start(bf16[2,8,128,128]{3,2,1,0:T(8,128)(2,1)S(1)} %add.52.refs_0_), channel_id=1, source_target_pairs={{0,2},{1,5},{2,0},{3,7},{4,6},{5,1},{6,4},{7,3},{8,10},{9,13},{10,... | collective-permute-start | bytes 1572872 | tf_op jit(solution)/shard_map/ppermute | solution.py:267
  26.0 12.5 %collective-permute-start.3 = (bf16[1,8,128,128]{3,2,1,0:T(8,128)(2,1)S(1)}, bf16[1,8,128,128]{3,2,1,0:T(8,128)(2,1)S(1)}, u32[]{:S(2)}, u32[]{:S(2)}) collective-permute-start(bf16[1,8,128,128]{3,2,1,0:T(8,128)(2,1)S(1)} %add.53.refs_3_), channel_id=1, source_target_pairs={{0,4},{1,3},{2,6},{3,1},{4,0},{5,7},{6,2},{7,5},{8,12},{9,11},{10,... | collective-permute-start | bytes 786440 | tf_op jit(solution)/shard_map/ppermute | solution.py:267
  38.7 9.3 %collective-permute-start.5 = (bf16[8,32,128]{2,1,0:T(8,128)(2,1)S(1)}, bf16[8,32,128]{2,1,0:T(8,128)(2,1)S(1)}, u32[]{:S(2)}, u32[]{:S(2)}) collective-permute-start(bf16[8,32,128]{2,1,0:T(8,128)(2,1)S(1)} %get-tuple-element.76), channel_id=1, source_target_pairs={{0,8},{8,0},{16,24},{24,16},{1,9},{9,1},{17,25},{25,17},{2,10},{10... | collective-permute-start | bytes 196616 | tf_op jit(solution)/shard_map/ppermute | solution.py:270
  43.5 12.9 %collective-permute-start.12 = (bf16[8,32,128]{2,1,0:T(8,128)(2,1)S(1)}, bf16[8,32,128]{2,1,0:T(8,128)(2,1)S(1)}, u32[]{:S(2)}, u32[]{:S(2)}) collective-permute-start(bf16[8,32,128]{2,1,0:T(8,128)(2,1)S(1)} %get-tuple-element.85), channel_id=1, source_target_pairs={{0,8},{8,0},{16,24},{24,16},{1,9},{9,1},{17,25},{25,17},{2,10},{10... | collective-permute-start | bytes 196616 | tf_op jit(solution)/shard_map/ppermute | solution.py:270
  45.1 12.7 %collective-permute-start.13 = (bf16[8,32,128]{2,1,0:T(8,128)(2,1)S(1)}, bf16[8,32,128]{2,1,0:T(8,128)(2,1)S(1)}, u32[]{:S(2)}, u32[]{:S(2)}) collective-permute-start(bf16[8,32,128]{2,1,0:T(8,128)(2,1)S(1)} %get-tuple-element.86), channel_id=1, source_target_pairs={{0,16},{8,24},{16,0},{24,8},{1,17},{9,25},{17,1},{25,9},{2,18},{10... | collective-permute-start | bytes 196616 | tf_op jit(solution)/shard_map/ppermute | solution.py:270
  48.0 9.9 %collective-permute-start.14 = (bf16[8,32,128]{2,1,0:T(8,128)(2,1)S(1)}, bf16[8,32,128]{2,1,0:T(8,128)(2,1)S(1)}, u32[]{:S(2)}, u32[]{:S(2)}) collective-permute-start(bf16[8,32,128]{2,1,0:T(8,128)(2,1)S(1)} %get-tuple-element.87), channel_id=1, source_target_pairs={{0,24},{8,16},{16,8},{24,0},{1,25},{9,17},{17,9},{25,1},{2,26},{10... | collective-permute-start | bytes 196616 | tf_op jit(solution)/shard_map/ppermute | solution.py:270
  51.0 11.0 %collective-permute-start.9 = (bf16[8,32,128]{2,1,0:T(8,128)(2,1)S(1)}, bf16[8,32,128]{2,1,0:T(8,128)(2,1)S(1)}, u32[]{:S(2)}, u32[]{:S(2)}) collective-permute-start(bf16[8,32,128]{2,1,0:T(8,128)(2,1)S(1)} %get-tuple-element.81), channel_id=1, source_target_pairs={{0,8},{8,0},{16,24},{24,16},{1,9},{9,1},{17,25},{25,17},{2,10},{10... | collective-permute-start | bytes 196616 | tf_op jit(solution)/shard_map/ppermute | solution.py:270
  54.3 9.1 %collective-permute-start.10 = (bf16[8,32,128]{2,1,0:T(8,128)(2,1)S(1)}, bf16[8,32,128]{2,1,0:T(8,128)(2,1)S(1)}, u32[]{:S(2)}, u32[]{:S(2)}) collective-permute-start(bf16[8,32,128]{2,1,0:T(8,128)(2,1)S(1)} %get-tuple-element.82), channel_id=1, source_target_pairs={{0,16},{8,24},{16,0},{24,8},{1,17},{9,25},{17,1},{25,9},{2,18},{10... | collective-permute-start | bytes 196616 | tf_op jit(solution)/shard_map/ppermute | solution.py:270
  70.4 9.2 %collective-permute-start.19 = (bf16[2,8,128,128]{3,2,1,0:T(8,128)(2,1)S(1)}, bf16[2,8,128,128]{3,2,1,0:T(8,128)(2,1)S(1)}, u32[]{:S(2)}, u32[]{:S(2)}) collective-permute-start(bf16[2,8,128,128]{3,2,1,0:T(8,128)(2,1)S(1)} %add.55.refs_0_), channel_id=1, source_target_pairs={{0,2},{1,5},{2,0},{3,7},{4,6},{5,1},{6,4},{7,3},{8,10},{9,13},{10,... | collective-permute-start | bytes 1572872 | tf_op jit(solution)/shard_map/ppermute | solution.py:267
  73.0 15.1 %collective-permute-start.22 = (bf16[2,8,128,128]{3,2,1,0:T(8,128)(2,1)S(1)}, bf16[2,8,128,128]{3,2,1,0:T(8,128)(2,1)S(1)}, u32[]{:S(2)}, u32[]{:S(2)}) collective-permute-start(bf16[2,8,128,128]{3,2,1,0:T(8,128)(2,1)S(1)} %add.56.refs_0_), channel_id=1, source_target_pairs={{0,2},{1,5},{2,0},{3,7},{4,6},{5,1},{6,4},{7,3},{8,10},{9,13},{10,... | collective-permute-start | bytes 1572872 | tf_op jit(solution)/shard_map/ppermute | solution.py:267
  79.7 9.1 %collective-permute-start.21 = (bf16[1,8,128,128]{3,2,1,0:T(8,128)(2,1)S(1)}, bf16[1,8,128,128]{3,2,1,0:T(8,128)(2,1)S(1)}, u32[]{:S(2)}, u32[]{:S(2)}) collective-permute-start(bf16[1,8,128,128]{3,2,1,0:T(8,128)(2,1)S(1)} %add.57.refs_3_), channel_id=1, source_target_pairs={{0,4},{1,3},{2,6},{3,1},{4,0},{5,7},{6,2},{7,5},{8,12},{9,11},{10,... | collective-permute-start | bytes 786440 | tf_op jit(solution)/shard_map/ppermute | solution.py:267
  89.7 9.5 %collective-permute-start.24 = (bf16[8,32,128]{2,1,0:T(8,128)(2,1)S(1)}, bf16[8,32,128]{2,1,0:T(8,128)(2,1)S(1)}, u32[]{:S(2)}, u32[]{:S(2)}) collective-permute-start(bf16[8,32,128]{2,1,0:T(8,128)(2,1)S(1)} %get-tuple-element.95), channel_id=1, source_target_pairs={{0,16},{8,24},{16,0},{24,8},{1,17},{9,25},{17,1},{25,9},{2,18},{10... | collective-permute-start | bytes 196616 | tf_op jit(solution)/shard_map/ppermute | solution.py:270
  94.8 9.9 %collective-permute-start.31 = (bf16[8,32,128]{2,1,0:T(8,128)(2,1)S(1)}, bf16[8,32,128]{2,1,0:T(8,128)(2,1)S(1)}, u32[]{:S(2)}, u32[]{:S(2)}) collective-permute-start(bf16[8,32,128]{2,1,0:T(8,128)(2,1)S(1)} %get-tuple-element.103), channel_id=1, source_target_pairs={{0,16},{8,24},{16,0},{24,8},{1,17},{9,25},{17,1},{25,9},{2,18},{10... | collective-permute-start | bytes 196616 | tf_op jit(solution)/shard_map/ppermute | solution.py:270
  117.1 9.2 %collective-permute-start.37 = (bf16[2,8,128,128]{3,2,1,0:T(8,128)(2,1)S(1)}, bf16[2,8,128,128]{3,2,1,0:T(8,128)(2,1)S(1)}, u32[]{:S(2)}, u32[]{:S(2)}) collective-permute-start(bf16[2,8,128,128]{3,2,1,0:T(8,128)(2,1)S(1)} %add.59.refs_0_), channel_id=1, source_target_pairs={{0,2},{1,5},{2,0},{3,7},{4,6},{5,1},{6,4},{7,3},{8,10},{9,13},{10,... | collective-permute-start | bytes 1572872 | tf_op jit(solution)/shard_map/ppermute | solution.py:267
  119.5 15.2 %collective-permute-start.40 = (bf16[2,8,128,128]{3,2,1,0:T(8,128)(2,1)S(1)}, bf16[2,8,128,128]{3,2,1,0:T(8,128)(2,1)S(1)}, u32[]{:S(2)}, u32[]{:S(2)}) collective-permute-start(bf16[2,8,128,128]{3,2,1,0:T(8,128)(2,1)S(1)} %add.60.refs_3_), channel_id=1, source_target_pairs={{0,2},{1,5},{2,0},{3,7},{4,6},{5,1},{6,4},{7,3},{8,10},{9,13},{10,... | collective-permute-start | bytes 1572872 | tf_op jit(solution)/shard_map/ppermute | solution.py:267
  126.4 9.2 %collective-permute-start.39 = (bf16[1,8,128,128]{3,2,1,0:T(8,128)(2,1)S(1)}, bf16[1,8,128,128]{3,2,1,0:T(8,128)(2,1)S(1)}, u32[]{:S(2)}, u32[]{:S(2)}) collective-permute-start(bf16[1,8,128,128]{3,2,1,0:T(8,128)(2,1)S(1)} %add.61.refs_3_), channel_id=1, source_target_pairs={{0,4},{1,3},{2,6},{3,1},{4,0},{5,7},{6,2},{7,5},{8,12},{9,11},{10,... | collective-permute-start | bytes 786440 | tf_op jit(solution)/shard_map/ppermute | solution.py:267
  137.0 9.2 %collective-permute-start.42 = (bf16[8,32,128]{2,1,0:T(8,128)(2,1)S(1)}, bf16[8,32,128]{2,1,0:T(8,128)(2,1)S(1)}, u32[]{:S(2)}, u32[]{:S(2)}) collective-permute-start(bf16[8,32,128]{2,1,0:T(8,128)(2,1)S(1)} %get-tuple-element.112), channel_id=1, source_target_pairs={{0,16},{8,24},{16,0},{24,8},{1,17},{9,25},{17,1},{25,9},{2,18},{10... | collective-permute-start | bytes 196616 | tf_op jit(solution)/shard_map/ppermute | solution.py:270
  143.3 8.8 %collective-permute-start.49 = (bf16[8,32,128]{2,1,0:T(8,128)(2,1)S(1)}, bf16[8,32,128]{2,1,0:T(8,128)(2,1)S(1)}, u32[]{:S(2)}, u32[]{:S(2)}) collective-permute-start(bf16[8,32,128]{2,1,0:T(8,128)(2,1)S(1)} %get-tuple-element.120), channel_id=1, source_target_pairs={{0,16},{8,24},{16,0},{24,8},{1,17},{9,25},{17,1},{25,9},{2,18},{10... | collective-permute-start | bytes 196616 | tf_op jit(solution)/shard_map/ppermute | solution.py:270
  147.3 11.5 %collective-permute-start.45 = (bf16[8,32,128]{2,1,0:T(8,128)(2,1)S(1)}, bf16[8,32,128]{2,1,0:T(8,128)(2,1)S(1)}, u32[]{:S(2)}, u32[]{:S(2)}) collective-permute-start(bf16[8,32,128]{2,1,0:T(8,128)(2,1)S(1)} %get-tuple-element.116), channel_id=1, source_target_pairs={{0,8},{8,0},{16,24},{24,16},{1,9},{9,1},{17,25},{25,17},{2,10},{10... | collective-permute-start | bytes 196616 | tf_op jit(solution)/shard_map/ppermute | solution.py:270
  149.3 10.7 %collective-permute-start.46 = (bf16[8,32,128]{2,1,0:T(8,128)(2,1)S(1)}, bf16[8,32,128]{2,1,0:T(8,128)(2,1)S(1)}, u32[]{:S(2)}, u32[]{:S(2)}) collective-permute-start(bf16[8,32,128]{2,1,0:T(8,128)(2,1)S(1)} %get-tuple-element.117), channel_id=1, source_target_pairs={{0,16},{8,24},{16,0},{24,8},{1,17},{9,25},{17,1},{25,9},{2,18},{10... | collective-permute-start | bytes 196616 | tf_op jit(solution)/shard_map/ppermute | solution.py:270
  149.9 10.1 %collective-permute-start.47 = (bf16[8,32,128]{2,1,0:T(8,128)(2,1)S(1)}, bf16[8,32,128]{2,1,0:T(8,128)(2,1)S(1)}, u32[]{:S(2)}, u32[]{:S(2)}) collective-permute-start(bf16[8,32,128]{2,1,0:T(8,128)(2,1)S(1)} %get-tuple-element.118), channel_id=1, source_target_pairs={{0,24},{8,16},{16,8},{24,0},{1,25},{9,17},{17,9},{25,1},{2,26},{10... | collective-permute-start | bytes 196616 | tf_op jit(solution)/shard_map/ppermute | solution.py:270
  153.3 10.5 %collective-permute-start.51 = (bf16[8,32,128]{2,1,0:T(8,128)(2,1)S(1)}, bf16[8,32,128]{2,1,0:T(8,128)(2,1)S(1)}, u32[]{:S(2)}, u32[]{:S(2)}) collective-permute-start(bf16[8,32,128]{2,1,0:T(8,128)(2,1)S(1)} %get-tuple-element.123), channel_id=1, source_target_pairs={{0,8},{8,0},{16,24},{24,16},{1,9},{9,1},{17,25},{25,17},{2,10},{10... | collective-permute-start | bytes 196616 | tf_op jit(solution)/shard_map/ppermute | solution.py:270
  167.0 9.2 %collective-permute-start.55 = (bf16[2,8,128,128]{3,2,1,0:T(8,128)(2,1)S(1)}, bf16[2,8,128,128]{3,2,1,0:T(8,128)(2,1)S(1)}, u32[]{:S(2)}, u32[]{:S(2)}) collective-permute-start(bf16[2,8,128,128]{3,2,1,0:T(8,128)(2,1)S(1)} %add.63.refs_0_), channel_id=1, source_target_pairs={{0,2},{1,5},{2,0},{3,7},{4,6},{5,1},{6,4},{7,3},{8,10},{9,13},{10,... | collective-permute-start | bytes 1572872 | tf_op jit(solution)/shard_map/ppermute | solution.py:267
  169.7 15.0 %collective-permute-start.58 = (bf16[2,8,128,128]{3,2,1,0:T(8,128)(2,1)S(1)}, bf16[2,8,128,128]{3,2,1,0:T(8,128)(2,1)S(1)}, u32[]{:S(2)}, u32[]{:S(2)}) collective-permute-start(bf16[2,8,128,128]{3,2,1,0:T(8,128)(2,1)S(1)} %add.64.refs_3_), channel_id=1, source_target_pairs={{0,2},{1,5},{2,0},{3,7},{4,6},{5,1},{6,4},{7,3},{8,10},{9,13},{10,... | collective-permute-start | bytes 1572872 | tf_op jit(solution)/shard_map/ppermute | solution.py:267
  176.4 9.7 %collective-permute-start.57 = (bf16[1,8,128,128]{3,2,1,0:T(8,128)(2,1)S(1)}, bf16[1,8,128,128]{3,2,1,0:T(8,128)(2,1)S(1)}, u32[]{:S(2)}, u32[]{:S(2)}) collective-permute-start(bf16[1,8,128,128]{3,2,1,0:T(8,128)(2,1)S(1)} %add.65.refs_3_), channel_id=1, source_target_pairs={{0,4},{1,3},{2,6},{3,1},{4,0},{5,7},{6,2},{7,5},{8,12},{9,11},{10,... | collective-permute-start | bytes 786440 | tf_op jit(solution)/shard_map/ppermute | solution.py:267
  187.7 8.8 %collective-permute-start.60 = (bf16[8,32,128]{2,1,0:T(8,128)(2,1)S(1)}, bf16[8,32,128]{2,1,0:T(8,128)(2,1)S(1)}, u32[]{:S(2)}, u32[]{:S(2)}) collective-permute-start(bf16[8,32,128]{2,1,0:T(8,128)(2,1)S(1)} %get-tuple-element.128), channel_id=1, source_target_pairs={{0,16},{8,24},{16,0},{24,8},{1,17},{9,25},{17,1},{25,9},{2,18},{10... | collective-permute-start | bytes 196616 | tf_op jit(solution)/shard_map/ppermute | solution.py:270
  191.4 9.6 %collective-permute-start.66 = (bf16[8,32,128]{2,1,0:T(8,128)(2,1)S(1)}, bf16[8,32,128]{2,1,0:T(8,128)(2,1)S(1)}, u32[]{:S(2)}, u32[]{:S(2)}) collective-permute-start(bf16[8,32,128]{2,1,0:T(8,128)(2,1)S(1)} %get-tuple-element.135), channel_id=1, source_target_pairs={{0,8},{8,0},{16,24},{24,16},{1,9},{9,1},{17,25},{25,17},{2,10},{10... | collective-permute-start | bytes 196616 | tf_op jit(solution)/shard_map/ppermute | solution.py:270
  192.1 11.3 %collective-permute-start.67 = (bf16[8,32,128]{2,1,0:T(8,128)(2,1)S(1)}, bf16[8,32,128]{2,1,0:T(8,128)(2,1)S(1)}, u32[]{:S(2)}, u32[]{:S(2)}) collective-permute-start(bf16[8,32,128]{2,1,0:T(8,128)(2,1)S(1)} %get-tuple-element.136), channel_id=1, source_target_pairs={{0,16},{8,24},{16,0},{24,8},{1,17},{9,25},{17,1},{25,9},{2,18},{10... | collective-permute-start | bytes 196616 | tf_op jit(solution)/shard_map/ppermute | solution.py:270
  194.2 9.2 %collective-permute-start.68 = (bf16[8,32,128]{2,1,0:T(8,128)(2,1)S(1)}, bf16[8,32,128]{2,1,0:T(8,128)(2,1)S(1)}, u32[]{:S(2)}, u32[]{:S(2)}) collective-permute-start(bf16[8,32,128]{2,1,0:T(8,128)(2,1)S(1)} %get-tuple-element.137), channel_id=1, source_target_pairs={{0,24},{8,16},{16,8},{24,0},{1,25},{9,17},{17,9},{25,1},{2,26},{10... | collective-permute-start | bytes 196616 | tf_op jit(solution)/shard_map/ppermute | solution.py:270
  197.6 8.9 %collective-permute-start.63 = (bf16[8,32,128]{2,1,0:T(8,128)(2,1)S(1)}, bf16[8,32,128]{2,1,0:T(8,128)(2,1)S(1)}, u32[]{:S(2)}, u32[]{:S(2)}) collective-permute-start(bf16[8,32,128]{2,1,0:T(8,128)(2,1)S(1)} %get-tuple-element.132), channel_id=1, source_target_pairs={{0,8},{8,0},{16,24},{24,16},{1,9},{9,1},{17,25},{25,17},{2,10},{10... | collective-permute-start | bytes 196616 | tf_op jit(solution)/shard_map/ppermute | solution.py:270
  (52 other events, 315.5 us)
where the time goes:
time: 215 us; the launch traced here: 214 us
  starting transfers between devices  96.7 us (45%)
  waiting for transfers between devices  58.5 us (27%)
  Pallas kernels  47.7 us (22%)
  local copies, waits for them, and re-layouts  10.2 us (5%)
    ppermute x48, starting transfers between devices, to_group(): return lax.ppermute(value, 'freq', [(z, z ^ k) for z in range(self.n_f)])  77.8 us
    ppermute x16, waiting for transfers between devices, to_chip(): return lax.ppermute(value, 'src', pairs)  47.5 us
    pallas_call x16, Pallas kernels, terms(): pl.pallas_call(functools.partial(terms_kernel, self.chunks, sign), out_sh...  30.6 us
    ppermute x16, starting transfers between devices, to_chip(): return lax.ppermute(value, 'src', pairs)  17.8 us
    unnamed x24, local copies, waits for them, and re-layouts  10.2 us
    ppermute x48, waiting for transfers between devices, to_group(): return lax.ppermute(value, 'freq', [(z, z ^ k) for z in range(self.n_f)])  9.29 us
    pallas_call x8, Pallas kernels, window(): pl.pallas_call(functools.partial(window_kernel, self.chunks, self.n_f, mi...  8.64 us
  transfers between devices with their start and end apart: 72, of which 25 were waited for; matrix products, arithmetic and copies ran while one was open for 0% of the time, Pallas kernels for 20%

commit v1 on v0

--- a/solution.py
+++ b/solution.py
@@ -18,6 +18,8 @@
 WEIGHT = 3e9
 UNROLL = 8
 BYTES = MIB
+ORDER = "00011011"
+START = "000111"
 TILE = 16
 PAD = 4
 TERMS_MIB = 32
@@ -437,13 +439,10 @@
     plan = Plan(reflection, direct_wave)
     plus = plan.pack(direct_wave)
     chains = [Chain(plan, i, plus[i]) for i in range(plan.chunks)]
-    first, second = chains[0], chains[-1]
     after = []
     for step in range(2 * ITERS):
-        for place, chain in enumerate([first, first, second, first, second, second]):
-            if step and place in (0, 2):
-                after = chain.step(after)
-            after = chain.step(after)
+        for i in ORDER if step else START:
+            after = chains[int(i)].step(after)
         if step == 0:
             after = plan.make_limits(first_arrival, after)
         if step == 1:

time: 215 us -> 212 us (0.986)
  starting transfers between devices: 96.7 us -> 102 us
  waiting for transfers between devices: 58.5 us -> 53.4 us
  local copies, waits for them, and re-layouts: 10.2 us -> 8.03 us
    ppermute x16, starting transfers between devices: 17.8 us -> 22.1 us  [to_chip(): return lax.ppermute(value, 'src', pairs)]
    ppermute x16, waiting for transfers between devices: 47.5 us -> 44.8 us  [to_chip(): return lax.ppermute(value, 'src', pairs)]
    unnamed x24 -> x26, local copies, waits for them, and re-layouts: 10.2 us -> 8.03 us
  transfers between devices with their start and end apart: 72 -> 72, of which waited for: 25 -> 24; matrix products, arithmetic and copies ran while one was open for 0% -> 0% of each run, Pallas kernels for 20% -> 19%
where the time goes in v1:
time: 212 us; the launch traced here: 211 us
  starting transfers between devices  102 us (48%)
  waiting for transfers between devices  53.4 us (25%)
  Pallas kernels  46.8 us (22%)
  local copies, waits for them, and re-layouts  8.03 us (4%)
    ppermute x48, starting transfers between devices, to_group(): return lax.ppermute(value, 'freq', [(z, z ^ k) for z in range(self.n_f)])  77.3 us
    ppermute x16, waiting for transfers between devices, to_chip(): return lax.ppermute(value, 'src', pairs)  44.8 us
    pallas_call x16, Pallas kernels, terms(): pl.pallas_call(functools.partial(terms_kernel, self.chunks, sign), out_sh...  29.6 us
    ppermute x16, starting transfers between devices, to_chip(): return lax.ppermute(value, 'src', pairs)  22.1 us
    pallas_call x8, Pallas kernels, window(): pl.pallas_call(functools.partial(window_kernel, self.chunks, self.n_f, mi...  8.67 us
    unnamed x26, local copies, waits for them, and re-layouts  8.03 us
    ppermute x48, waiting for transfers between devices, to_group(): return lax.ppermute(value, 'freq', [(z, z ^ k) for z in range(self.n_f)])  7.68 us
  transfers between devices with their start and end apart: 72, of which 24 were waited for; matrix products, arithmetic and copies ran while one was open for 0% of the time, Pallas kernels for 19%

profile of v1, /device:TPU:0, one launch (start us, length us, event | category | flops | bytes accessed | tf_op | source)
XLA Modules:
  0.0 211.5 jit_solution(18404527083372148192)
XLA Ops:
  3.0 3.4 %copy-done.2 = bf16[2,16,1024,128]{3,2,1,0:T(8,128)(2,1)S(1)} copy-done((bf16[2,16,1024,128]{3,2,1,0:T(8,128)(2,1)S(1)}, bf16[2,16,1024,128]{3,2,1,0:T(8,128)(2,1)}, u32[]{:S(2)}) %copy-start.2) | copy-done | bytes 8388632
  13.5 2.6 %collective-permute-start.2 = (bf16[2,8,128,128]{3,2,1,0:T(8,128)(2,1)}, bf16[2,8,128,128]{3,2,1,0:T(8,128)(2,1)S(1)}, u32[]{:S(2)}, u32[]{:S(2)}) collective-permute-start(bf16[2,8,128,128]{3,2,1,0:T(8,128)(2,1)} %copy-done.4), channel_id=1, source_target_pairs={{0,2},{1,5},{2,0},{3,7},{4,6},{5,1},{6,4},{7,3},{8,10},{9,13},{10,... | collective-permute-start | bytes 1572872 | tf_op jit(solution)/shard_map/ppermute | solution.py:269
  16.1 3.4 %copy-done.3 = bf16[2,16,1024,128]{3,2,1,0:T(8,128)(2,1)S(1)} copy-done((bf16[2,16,1024,128]{3,2,1,0:T(8,128)(2,1)S(1)}, bf16[2,16,1024,128]{3,2,1,0:T(8,128)(2,1)}, u32[]{:S(2)}) %copy-start.3) | copy-done | bytes 8388632
  23.6 2.1 collective-permute-start.3
  25.7 7.9 %collective-permute-done.4.refs_2_ = bf16[2,8,128,128]{3,2,1,0:T(8,128)(2,1)S(1)} collective-permute-done((bf16[2,8,128,128]{3,2,1,0:T(8,128)(2,1)S(1)}, bf16[2,8,128,128]{3,2,1,0:T(8,128)(2,1)S(1)}, u32[]{:S(2)}, u32[]{:S(2)}) %collective-permute-start.4) | collective-permute-done | bytes 524320 | tf_op jit(solution)/shard_map/ppermute | solution.py:269
  35.5 1.9 collective-permute-start.5
  37.4 2.6 %collective-permute-start.6 = (bf16[8,32,128]{2,1,0:T(8,128)(2,1)S(1)}, bf16[8,32,128]{2,1,0:T(8,128)(2,1)S(1)}, u32[]{:S(2)}, u32[]{:S(2)}) collective-permute-start(bf16[8,32,128]{2,1,0:T(8,128)(2,1)S(1)} %get-tuple-element.77), channel_id=1, source_target_pairs={{0,16},{8,24},{16,0},{24,8},{1,17},{9,25},{17,1},{25,9},{2,18},{10... | collective-permute-start | bytes 196616 | tf_op jit(solution)/shard_map/ppermute | solution.py:272
  41.9 2.7 %collective-permute-start.13 = (bf16[8,32,128]{2,1,0:T(8,128)(2,1)S(1)}, bf16[8,32,128]{2,1,0:T(8,128)(2,1)S(1)}, u32[]{:S(2)}, u32[]{:S(2)}) collective-permute-start(bf16[8,32,128]{2,1,0:T(8,128)(2,1)S(1)} %get-tuple-element.86), channel_id=1, source_target_pairs={{0,16},{8,24},{16,0},{24,8},{1,17},{9,25},{17,1},{25,9},{2,18},{10... | collective-permute-start | bytes 196616 | tf_op jit(solution)/shard_map/ppermute | solution.py:272
  47.2 2.4 %collective-permute-start.9 = (bf16[8,32,128]{2,1,0:T(8,128)(2,1)S(1)}, bf16[8,32,128]{2,1,0:T(8,128)(2,1)S(1)}, u32[]{:S(2)}, u32[]{:S(2)}) collective-permute-start(bf16[8,32,128]{2,1,0:T(8,128)(2,1)S(1)} %get-tuple-element.81), channel_id=1, source_target_pairs={{0,8},{8,0},{16,24},{24,16},{1,9},{9,1},{17,25},{25,17},{2,10},{10... | collective-permute-start | bytes 196616 | tf_op jit(solution)/shard_map/ppermute | solution.py:272
  69.4 4.1 %collective-permute-done.19.refs_2_ = bf16[2,8,128,128]{3,2,1,0:T(8,128)(2,1)S(1)} collective-permute-done((bf16[2,8,128,128]{3,2,1,0:T(8,128)(2,1)S(1)}, bf16[2,8,128,128]{3,2,1,0:T(8,128)(2,1)S(1)}, u32[]{:S(2)}, u32[]{:S(2)}) %collective-permute-start.19) | collective-permute-done | bytes 524320 | tf_op jit(solution)/shard_map/ppermute | solution.py:269
  73.6 1.9 collective-permute-start.21
  75.5 6.4 %collective-permute-done.22.refs_2_ = bf16[2,8,128,128]{3,2,1,0:T(8,128)(2,1)S(1)} collective-permute-done((bf16[2,8,128,128]{3,2,1,0:T(8,128)(2,1)S(1)}, bf16[2,8,128,128]{3,2,1,0:T(8,128)(2,1)S(1)}, u32[]{:S(2)}, u32[]{:S(2)}) %collective-permute-start.22) | collective-permute-done | bytes 524320 | tf_op jit(solution)/shard_map/ppermute | solution.py:269
  86.6 2.0 collective-permute-start.25
  91.2 2.0 collective-permute-start.32
  95.0 4.8 %collective-permute-start.27 = (bf16[8,32,128]{2,1,0:T(8,128)(2,1)S(1)}, bf16[8,32,128]{2,1,0:T(8,128)(2,1)S(1)}, u32[]{:S(2)}, u32[]{:S(2)}) collective-permute-start(bf16[8,32,128]{2,1,0:T(8,128)(2,1)S(1)} %get-tuple-element.99), channel_id=1, source_target_pairs={{0,8},{8,0},{16,24},{24,16},{1,9},{9,1},{17,25},{25,17},{2,10},{10... | collective-permute-start | bytes 196616 | tf_op jit(solution)/shard_map/ppermute | solution.py:272
  99.8 2.4 %collective-permute-start.29 = (bf16[8,32,128]{2,1,0:T(8,128)(2,1)S(1)}, bf16[8,32,128]{2,1,0:T(8,128)(2,1)S(1)}, u32[]{:S(2)}, u32[]{:S(2)}) collective-permute-start(bf16[8,32,128]{2,1,0:T(8,128)(2,1)S(1)} %get-tuple-element.101), channel_id=1, source_target_pairs={{0,24},{8,16},{16,8},{24,0},{1,25},{9,17},{17,9},{25,1},{2,26},{10... | collective-permute-start | bytes 196616 | tf_op jit(solution)/shard_map/ppermute | solution.py:272
  105.4 2.4 %collective-permute-start.36 = (bf16[8,32,128]{2,1,0:T(8,128)(2,1)S(1)}, bf16[8,32,128]{2,1,0:T(8,128)(2,1)S(1)}, u32[]{:S(2)}, u32[]{:S(2)}) collective-permute-start(bf16[8,32,128]{2,1,0:T(8,128)(2,1)S(1)} %get-tuple-element.108), channel_id=1, source_target_pairs={{0,24},{8,16},{16,8},{24,0},{1,25},{9,17},{17,9},{25,1},{2,26},{10... | collective-permute-start | bytes 196616 | tf_op jit(solution)/shard_map/ppermute | solution.py:272
  116.6 2.0 collective-permute-start.40
  118.6 5.1 %collective-permute-done.37.refs_2_ = bf16[2,8,128,128]{3,2,1,0:T(8,128)(2,1)S(1)} collective-permute-done((bf16[2,8,128,128]{3,2,1,0:T(8,128)(2,1)S(1)}, bf16[2,8,128,128]{3,2,1,0:T(8,128)(2,1)S(1)}, u32[]{:S(2)}, u32[]{:S(2)}) %collective-permute-start.37) | collective-permute-done | bytes 524320 | tf_op jit(solution)/shard_map/ppermute | solution.py:269
  123.9 8.2 %collective-permute-done.40.refs_2_ = bf16[2,8,128,128]{3,2,1,0:T(8,128)(2,1)S(1)} collective-permute-done((bf16[2,8,128,128]{3,2,1,0:T(8,128)(2,1)S(1)}, bf16[2,8,128,128]{3,2,1,0:T(8,128)(2,1)S(1)}, u32[]{:S(2)}, u32[]{:S(2)}) %collective-permute-start.40) | collective-permute-done | bytes 524320 | tf_op jit(solution)/shard_map/ppermute | solution.py:269
  134.7 2.3 %collective-permute-start.43 = (bf16[8,32,128]{2,1,0:T(8,128)(2,1)S(1)}, bf16[8,32,128]{2,1,0:T(8,128)(2,1)S(1)}, u32[]{:S(2)}, u32[]{:S(2)}) collective-permute-start(bf16[8,32,128]{2,1,0:T(8,128)(2,1)S(1)} %get-tuple-element.113), channel_id=1, source_target_pairs={{0,24},{8,16},{16,8},{24,0},{1,25},{9,17},{17,9},{25,1},{2,26},{10... | collective-permute-start | bytes 196616 | tf_op jit(solution)/shard_map/ppermute | solution.py:272
  141.0 2.3 %collective-permute-start.50 = (bf16[8,32,128]{2,1,0:T(8,128)(2,1)S(1)}, bf16[8,32,128]{2,1,0:T(8,128)(2,1)S(1)}, u32[]{:S(2)}, u32[]{:S(2)}) collective-permute-start(bf16[8,32,128]{2,1,0:T(8,128)(2,1)S(1)} %get-tuple-element.121), channel_id=1, source_target_pairs={{0,24},{8,16},{16,8},{24,0},{1,25},{9,17},{17,9},{25,1},{2,26},{10... | collective-permute-start | bytes 196616 | tf_op jit(solution)/shard_map/ppermute | solution.py:272
  146.6 2.3 %collective-permute-start.47 = (bf16[8,32,128]{2,1,0:T(8,128)(2,1)S(1)}, bf16[8,32,128]{2,1,0:T(8,128)(2,1)S(1)}, u32[]{:S(2)}, u32[]{:S(2)}) collective-permute-start(bf16[8,32,128]{2,1,0:T(8,128)(2,1)S(1)} %get-tuple-element.118), channel_id=1, source_target_pairs={{0,24},{8,16},{16,8},{24,0},{1,25},{9,17},{17,9},{25,1},{2,26},{10... | collective-permute-start | bytes 196616 | tf_op jit(solution)/shard_map/ppermute | solution.py:272
  152.1 2.3 %collective-permute-start.53 = (bf16[8,32,128]{2,1,0:T(8,128)(2,1)S(1)}, bf16[8,32,128]{2,1,0:T(8,128)(2,1)S(1)}, u32[]{:S(2)}, u32[]{:S(2)}) collective-permute-start(bf16[8,32,128]{2,1,0:T(8,128)(2,1)S(1)} %get-tuple-element.125), channel_id=1, source_target_pairs={{0,24},{8,16},{16,8},{24,0},{1,25},{9,17},{17,9},{25,1},{2,26},{10... | collective-permute-start | bytes 196616 | tf_op jit(solution)/shard_map/ppermute | solution.py:272
  161.0 3.1 %collective-permute-start.55 = (bf16[2,8,128,128]{3,2,1,0:T(8,128)(2,1)S(1)}, bf16[2,8,128,128]{3,2,1,0:T(8,128)(2,1)S(1)}, u32[]{:S(2)}, u32[]{:S(2)}) collective-permute-start(bf16[2,8,128,128]{3,2,1,0:T(8,128)(2,1)S(1)} %add.63.refs_0_), channel_id=1, source_target_pairs={{0,2},{1,5},{2,0},{3,7},{4,6},{5,1},{6,4},{7,3},{8,10},{9,13},{10,... | collective-permute-start | bytes 1572872 | tf_op jit(solution)/shard_map/ppermute | solution.py:269
  168.3 3.0 %collective-permute-done.55.refs_2_ = bf16[2,8,128,128]{3,2,1,0:T(8,128)(2,1)S(1)} collective-permute-done((bf16[2,8,128,128]{3,2,1,0:T(8,128)(2,1)S(1)}, bf16[2,8,128,128]{3,2,1,0:T(8,128)(2,1)S(1)}, u32[]{:S(2)}, u32[]{:S(2)}) %collective-permute-start.55) | collective-permute-done | bytes 524320 | tf_op jit(solution)/shard_map/ppermute | solution.py:269
  173.2 6.4 %collective-permute-done.58.refs_2_ = bf16[2,8,128,128]{3,2,1,0:T(8,128)(2,1)S(1)} collective-permute-done((bf16[2,8,128,128]{3,2,1,0:T(8,128)(2,1)S(1)}, bf16[2,8,128,128]{3,2,1,0:T(8,128)(2,1)S(1)}, u32[]{:S(2)}, u32[]{:S(2)}) %collective-permute-start.58) | collective-permute-done | bytes 524320 | tf_op jit(solution)/shard_map/ppermute | solution.py:269
  183.9 2.3 %collective-permute-start.61 = (bf16[8,32,128]{2,1,0:T(8,128)(2,1)S(1)}, bf16[8,32,128]{2,1,0:T(8,128)(2,1)S(1)}, u32[]{:S(2)}, u32[]{:S(2)}) collective-permute-start(bf16[8,32,128]{2,1,0:T(8,128)(2,1)S(1)} %get-tuple-element.129), channel_id=1, source_target_pairs={{0,24},{8,16},{16,8},{24,0},{1,25},{9,17},{17,9},{25,1},{2,26},{10... | collective-permute-start | bytes 196616 | tf_op jit(solution)/shard_map/ppermute | solution.py:272
  193.0 4.8 %collective-permute-start.63 = (bf16[8,32,128]{2,1,0:T(8,128)(2,1)S(1)}, bf16[8,32,128]{2,1,0:T(8,128)(2,1)S(1)}, u32[]{:S(2)}, u32[]{:S(2)}) collective-permute-start(bf16[8,32,128]{2,1,0:T(8,128)(2,1)S(1)} %get-tuple-element.132), channel_id=1, source_target_pairs={{0,8},{8,0},{16,24},{24,16},{1,9},{9,1},{17,25},{25,17},{2,10},{10... | collective-permute-start | bytes 196616 | tf_op jit(solution)/shard_map/ppermute | solution.py:272
  198.0 2.2 %collective-permute-start.65 = (bf16[8,32,128]{2,1,0:T(8,128)(2,1)S(1)}, bf16[8,32,128]{2,1,0:T(8,128)(2,1)S(1)}, u32[]{:S(2)}, u32[]{:S(2)}) collective-permute-start(bf16[8,32,128]{2,1,0:T(8,128)(2,1)S(1)} %get-tuple-element.134), channel_id=1, source_target_pairs={{0,24},{8,16},{16,8},{24,0},{1,25},{9,17},{17,9},{25,1},{2,26},{10... | collective-permute-start | bytes 196616 | tf_op jit(solution)/shard_map/ppermute | solution.py:272
  203.6 2.2 %collective-permute-start.71 = (bf16[8,32,128]{2,1,0:T(8,128)(2,1)S(1)}, bf16[8,32,128]{2,1,0:T(8,128)(2,1)S(1)}, u32[]{:S(2)}, u32[]{:S(2)}) collective-permute-start(bf16[8,32,128]{2,1,0:T(8,128)(2,1)S(1)} %get-tuple-element.141), channel_id=1, source_target_pairs={{0,24},{8,16},{16,8},{24,0},{1,25},{9,17},{17,9},{25,1},{2,26},{10... | collective-permute-start | bytes 196616 | tf_op jit(solution)/shard_map/ppermute | solution.py:272
  206.1 2.3 %collective-permute-done.70.refs_2_ = bf16[8,32,128]{2,1,0:T(8,128)(2,1)S(1)} collective-permute-done((bf16[8,32,128]{2,1,0:T(8,128)(2,1)S(1)}, bf16[8,32,128]{2,1,0:T(8,128)(2,1)S(1)}, u32[]{:S(2)}, u32[]{:S(2)}) %collective-permute-start.70) | collective-permute-done | bytes 65568 | tf_op jit(solution)/shard_map/ppermute | solution.py:272
  (201 shorter events, 104.4 us)
Async XLA Ops:
  13.5 10.0 %collective-permute-start.2 = (bf16[2,8,128,128]{3,2,1,0:T(8,128)(2,1)}, bf16[2,8,128,128]{3,2,1,0:T(8,128)(2,1)S(1)}, u32[]{:S(2)}, u32[]{:S(2)}) collective-permute-start(bf16[2,8,128,128]{3,2,1,0:T(8,128)(2,1)} %copy-done.4), channel_id=1, source_target_pairs={{0,2},{1,5},{2,0},{3,7},{4,6},{5,1},{6,4},{7,3},{8,10},{9,13},{10,... | collective-permute-start | bytes 1572872 | tf_op jit(solution)/shard_map/ppermute | solution.py:269
  21.5 12.1 %collective-permute-start.4 = (bf16[2,8,128,128]{3,2,1,0:T(8,128)(2,1)S(1)}, bf16[2,8,128,128]{3,2,1,0:T(8,128)(2,1)S(1)}, u32[]{:S(2)}, u32[]{:S(2)}) collective-permute-start(bf16[2,8,128,128]{3,2,1,0:T(8,128)(2,1)S(1)} %add.52.refs_0_), channel_id=1, source_target_pairs={{0,2},{1,5},{2,0},{3,7},{4,6},{5,1},{6,4},{7,3},{8,10},{9,13},{10,... | collective-permute-start | bytes 1572872 | tf_op jit(solution)/shard_map/ppermute | solution.py:269
  23.6 11.7 %collective-permute-start.3 = (bf16[1,8,128,128]{3,2,1,0:T(8,128)(2,1)S(1)}, bf16[1,8,128,128]{3,2,1,0:T(8,128)(2,1)S(1)}, u32[]{:S(2)}, u32[]{:S(2)}) collective-permute-start(bf16[1,8,128,128]{3,2,1,0:T(8,128)(2,1)S(1)} %add.53.refs_3_), channel_id=1, source_target_pairs={{0,4},{1,3},{2,6},{3,1},{4,0},{5,7},{6,2},{7,5},{8,12},{9,11},{10,... | collective-permute-start | bytes 786440 | tf_op jit(solution)/shard_map/ppermute | solution.py:269
  35.5 9.1 %collective-permute-start.5 = (bf16[8,32,128]{2,1,0:T(8,128)(2,1)S(1)}, bf16[8,32,128]{2,1,0:T(8,128)(2,1)S(1)}, u32[]{:S(2)}, u32[]{:S(2)}) collective-permute-start(bf16[8,32,128]{2,1,0:T(8,128)(2,1)S(1)} %get-tuple-element.76), channel_id=1, source_target_pairs={{0,8},{8,0},{16,24},{24,16},{1,9},{9,1},{17,25},{25,17},{2,10},{10... | collective-permute-start | bytes 196616 | tf_op jit(solution)/shard_map/ppermute | solution.py:272
  40.2 9.9 %collective-permute-start.12 = (bf16[8,32,128]{2,1,0:T(8,128)(2,1)S(1)}, bf16[8,32,128]{2,1,0:T(8,128)(2,1)S(1)}, u32[]{:S(2)}, u32[]{:S(2)}) collective-permute-start(bf16[8,32,128]{2,1,0:T(8,128)(2,1)S(1)} %get-tuple-element.85), channel_id=1, source_target_pairs={{0,8},{8,0},{16,24},{24,16},{1,9},{9,1},{17,25},{25,17},{2,10},{10... | collective-permute-start | bytes 196616 | tf_op jit(solution)/shard_map/ppermute | solution.py:272
  41.9 10.2 %collective-permute-start.13 = (bf16[8,32,128]{2,1,0:T(8,128)(2,1)S(1)}, bf16[8,32,128]{2,1,0:T(8,128)(2,1)S(1)}, u32[]{:S(2)}, u32[]{:S(2)}) collective-permute-start(bf16[8,32,128]{2,1,0:T(8,128)(2,1)S(1)} %get-tuple-element.86), channel_id=1, source_target_pairs={{0,16},{8,24},{16,0},{24,8},{1,17},{9,25},{17,1},{25,9},{2,18},{10... | collective-permute-start | bytes 196616 | tf_op jit(solution)/shard_map/ppermute | solution.py:272
  47.2 8.5 %collective-permute-start.9 = (bf16[8,32,128]{2,1,0:T(8,128)(2,1)S(1)}, bf16[8,32,128]{2,1,0:T(8,128)(2,1)S(1)}, u32[]{:S(2)}, u32[]{:S(2)}) collective-permute-start(bf16[8,32,128]{2,1,0:T(8,128)(2,1)S(1)} %get-tuple-element.81), channel_id=1, source_target_pairs={{0,8},{8,0},{16,24},{24,16},{1,9},{9,1},{17,25},{25,17},{2,10},{10... | collective-permute-start | bytes 196616 | tf_op jit(solution)/shard_map/ppermute | solution.py:272
  64.3 9.2 %collective-permute-start.19 = (bf16[2,8,128,128]{3,2,1,0:T(8,128)(2,1)S(1)}, bf16[2,8,128,128]{3,2,1,0:T(8,128)(2,1)S(1)}, u32[]{:S(2)}, u32[]{:S(2)}) collective-permute-start(bf16[2,8,128,128]{3,2,1,0:T(8,128)(2,1)S(1)} %add.55.refs_0_), channel_id=1, source_target_pairs={{0,2},{1,5},{2,0},{3,7},{4,6},{5,1},{6,4},{7,3},{8,10},{9,13},{10,... | collective-permute-start | bytes 1572872 | tf_op jit(solution)/shard_map/ppermute | solution.py:269
  66.8 15.1 %collective-permute-start.22 = (bf16[2,8,128,128]{3,2,1,0:T(8,128)(2,1)S(1)}, bf16[2,8,128,128]{3,2,1,0:T(8,128)(2,1)S(1)}, u32[]{:S(2)}, u32[]{:S(2)}) collective-permute-start(bf16[2,8,128,128]{3,2,1,0:T(8,128)(2,1)S(1)} %add.56.refs_0_), channel_id=1, source_target_pairs={{0,2},{1,5},{2,0},{3,7},{4,6},{5,1},{6,4},{7,3},{8,10},{9,13},{10,... | collective-permute-start | bytes 1572872 | tf_op jit(solution)/shard_map/ppermute | solution.py:269
  73.6 10.4 %collective-permute-start.21 = (bf16[1,8,128,128]{3,2,1,0:T(8,128)(2,1)S(1)}, bf16[1,8,128,128]{3,2,1,0:T(8,128)(2,1)S(1)}, u32[]{:S(2)}, u32[]{:S(2)}) collective-permute-start(bf16[1,8,128,128]{3,2,1,0:T(8,128)(2,1)S(1)} %add.57.refs_3_), channel_id=1, source_target_pairs={{0,4},{1,3},{2,6},{3,1},{4,0},{5,7},{6,2},{7,5},{8,12},{9,11},{10,... | collective-permute-start | bytes 786440 | tf_op jit(solution)/shard_map/ppermute | solution.py:269
  85.2 8.7 %collective-permute-start.24 = (bf16[8,32,128]{2,1,0:T(8,128)(2,1)S(1)}, bf16[8,32,128]{2,1,0:T(8,128)(2,1)S(1)}, u32[]{:S(2)}, u32[]{:S(2)}) collective-permute-start(bf16[8,32,128]{2,1,0:T(8,128)(2,1)S(1)} %get-tuple-element.95), channel_id=1, source_target_pairs={{0,16},{8,24},{16,0},{24,8},{1,17},{9,25},{17,1},{25,9},{2,18},{10... | collective-permute-start | bytes 196616 | tf_op jit(solution)/shard_map/ppermute | solution.py:272
  88.7 11.1 %collective-permute-start.30 = (bf16[8,32,128]{2,1,0:T(8,128)(2,1)S(1)}, bf16[8,32,128]{2,1,0:T(8,128)(2,1)S(1)}, u32[]{:S(2)}, u32[]{:S(2)}) collective-permute-start(bf16[8,32,128]{2,1,0:T(8,128)(2,1)S(1)} %get-tuple-element.102), channel_id=1, source_target_pairs={{0,8},{8,0},{16,24},{24,16},{1,9},{9,1},{17,25},{25,17},{2,10},{10... | collective-permute-start | bytes 196616 | tf_op jit(solution)/shard_map/ppermute | solution.py:272
  89.6 12.7 %collective-permute-start.31 = (bf16[8,32,128]{2,1,0:T(8,128)(2,1)S(1)}, bf16[8,32,128]{2,1,0:T(8,128)(2,1)S(1)}, u32[]{:S(2)}, u32[]{:S(2)}) collective-permute-start(bf16[8,32,128]{2,1,0:T(8,128)(2,1)S(1)} %get-tuple-element.103), channel_id=1, source_target_pairs={{0,16},{8,24},{16,0},{24,8},{1,17},{9,25},{17,1},{25,9},{2,18},{10... | collective-permute-start | bytes 196616 | tf_op jit(solution)/shard_map/ppermute | solution.py:272
  91.2 11.1 %collective-permute-start.32 = (bf16[8,32,128]{2,1,0:T(8,128)(2,1)S(1)}, bf16[8,32,128]{2,1,0:T(8,128)(2,1)S(1)}, u32[]{:S(2)}, u32[]{:S(2)}) collective-permute-start(bf16[8,32,128]{2,1,0:T(8,128)(2,1)S(1)} %get-tuple-element.104), channel_id=1, source_target_pairs={{0,24},{8,16},{16,8},{24,0},{1,25},{9,17},{17,9},{25,1},{2,26},{10... | collective-permute-start | bytes 196616 | tf_op jit(solution)/shard_map/ppermute | solution.py:272
  95.0 10.4 %collective-permute-start.27 = (bf16[8,32,128]{2,1,0:T(8,128)(2,1)S(1)}, bf16[8,32,128]{2,1,0:T(8,128)(2,1)S(1)}, u32[]{:S(2)}, u32[]{:S(2)}) collective-permute-start(bf16[8,32,128]{2,1,0:T(8,128)(2,1)S(1)} %get-tuple-element.99), channel_id=1, source_target_pairs={{0,8},{8,0},{16,24},{24,16},{1,9},{9,1},{17,25},{25,17},{2,10},{10... | collective-permute-start | bytes 196616 | tf_op jit(solution)/shard_map/ppermute | solution.py:272
  103.4 8.3 %collective-permute-start.34 = (bf16[8,32,128]{2,1,0:T(8,128)(2,1)S(1)}, bf16[8,32,128]{2,1,0:T(8,128)(2,1)S(1)}, u32[]{:S(2)}, u32[]{:S(2)}) collective-permute-start(bf16[8,32,128]{2,1,0:T(8,128)(2,1)S(1)} %get-tuple-element.106), channel_id=1, source_target_pairs={{0,8},{8,0},{16,24},{24,16},{1,9},{9,1},{17,25},{25,17},{2,10},{10... | collective-permute-start | bytes 196616 | tf_op jit(solution)/shard_map/ppermute | solution.py:272
  114.5 9.2 %collective-permute-start.37 = (bf16[2,8,128,128]{3,2,1,0:T(8,128)(2,1)S(1)}, bf16[2,8,128,128]{3,2,1,0:T(8,128)(2,1)S(1)}, u32[]{:S(2)}, u32[]{:S(2)}) collective-permute-start(bf16[2,8,128,128]{3,2,1,0:T(8,128)(2,1)S(1)} %add.59.refs_0_), channel_id=1, source_target_pairs={{0,2},{1,5},{2,0},{3,7},{4,6},{5,1},{6,4},{7,3},{8,10},{9,13},{10,... | collective-permute-start | bytes 1572872 | tf_op jit(solution)/shard_map/ppermute | solution.py:269
  116.6 15.5 %collective-permute-start.40 = (bf16[2,8,128,128]{3,2,1,0:T(8,128)(2,1)S(1)}, bf16[2,8,128,128]{3,2,1,0:T(8,128)(2,1)S(1)}, u32[]{:S(2)}, u32[]{:S(2)}) collective-permute-start(bf16[2,8,128,128]{3,2,1,0:T(8,128)(2,1)S(1)} %add.60.refs_3_), channel_id=1, source_target_pairs={{0,2},{1,5},{2,0},{3,7},{4,6},{5,1},{6,4},{7,3},{8,10},{9,13},{10,... | collective-permute-start | bytes 1572872 | tf_op jit(solution)/shard_map/ppermute | solution.py:269
  123.8 8.5 %collective-permute-start.39 = (bf16[1,8,128,128]{3,2,1,0:T(8,128)(2,1)S(1)}, bf16[1,8,128,128]{3,2,1,0:T(8,128)(2,1)S(1)}, u32[]{:S(2)}, u32[]{:S(2)}) collective-permute-start(bf16[1,8,128,128]{3,2,1,0:T(8,128)(2,1)S(1)} %add.61.refs_3_), channel_id=1, source_target_pairs={{0,4},{1,3},{2,6},{3,1},{4,0},{5,7},{6,2},{7,5},{8,12},{9,11},{10,... | collective-permute-start | bytes 786440 | tf_op jit(solution)/shard_map/ppermute | solution.py:269
  132.5 8.5 %collective-permute-start.41 = (bf16[8,32,128]{2,1,0:T(8,128)(2,1)S(1)}, bf16[8,32,128]{2,1,0:T(8,128)(2,1)S(1)}, u32[]{:S(2)}, u32[]{:S(2)}) collective-permute-start(bf16[8,32,128]{2,1,0:T(8,128)(2,1)S(1)} %get-tuple-element.111), channel_id=1, source_target_pairs={{0,8},{8,0},{16,24},{24,16},{1,9},{9,1},{17,25},{25,17},{2,10},{10... | collective-permute-start | bytes 196616 | tf_op jit(solution)/shard_map/ppermute | solution.py:272
  133.2 10.1 %collective-permute-start.42 = (bf16[8,32,128]{2,1,0:T(8,128)(2,1)S(1)}, bf16[8,32,128]{2,1,0:T(8,128)(2,1)S(1)}, u32[]{:S(2)}, u32[]{:S(2)}) collective-permute-start(bf16[8,32,128]{2,1,0:T(8,128)(2,1)S(1)} %get-tuple-element.112), channel_id=1, source_target_pairs={{0,16},{8,24},{16,0},{24,8},{1,17},{9,25},{17,1},{25,9},{2,18},{10... | collective-permute-start | bytes 196616 | tf_op jit(solution)/shard_map/ppermute | solution.py:272
  134.7 8.6 %collective-permute-start.43 = (bf16[8,32,128]{2,1,0:T(8,128)(2,1)S(1)}, bf16[8,32,128]{2,1,0:T(8,128)(2,1)S(1)}, u32[]{:S(2)}, u32[]{:S(2)}) collective-permute-start(bf16[8,32,128]{2,1,0:T(8,128)(2,1)S(1)} %get-tuple-element.113), channel_id=1, source_target_pairs={{0,24},{8,16},{16,8},{24,0},{1,25},{9,17},{17,9},{25,1},{2,26},{10... | collective-permute-start | bytes 196616 | tf_op jit(solution)/shard_map/ppermute | solution.py:272
  139.5 9.3 %collective-permute-start.49 = (bf16[8,32,128]{2,1,0:T(8,128)(2,1)S(1)}, bf16[8,32,128]{2,1,0:T(8,128)(2,1)S(1)}, u32[]{:S(2)}, u32[]{:S(2)}) collective-permute-start(bf16[8,32,128]{2,1,0:T(8,128)(2,1)S(1)} %get-tuple-element.120), channel_id=1, source_target_pairs={{0,16},{8,24},{16,0},{24,8},{1,17},{9,25},{17,1},{25,9},{2,18},{10... | collective-permute-start | bytes 196616 | tf_op jit(solution)/shard_map/ppermute | solution.py:272
  145.4 9.0 %collective-permute-start.46 = (bf16[8,32,128]{2,1,0:T(8,128)(2,1)S(1)}, bf16[8,32,128]{2,1,0:T(8,128)(2,1)S(1)}, u32[]{:S(2)}, u32[]{:S(2)}) collective-permute-start(bf16[8,32,128]{2,1,0:T(8,128)(2,1)S(1)} %get-tuple-element.117), channel_id=1, source_target_pairs={{0,16},{8,24},{16,0},{24,8},{1,17},{9,25},{17,1},{25,9},{2,18},{10... | collective-permute-start | bytes 196616 | tf_op jit(solution)/shard_map/ppermute | solution.py:272
  161.0 10.2 %collective-permute-start.55 = (bf16[2,8,128,128]{3,2,1,0:T(8,128)(2,1)S(1)}, bf16[2,8,128,128]{3,2,1,0:T(8,128)(2,1)S(1)}, u32[]{:S(2)}, u32[]{:S(2)}) collective-permute-start(bf16[2,8,128,128]{3,2,1,0:T(8,128)(2,1)S(1)} %add.63.refs_0_), channel_id=1, source_target_pairs={{0,2},{1,5},{2,0},{3,7},{4,6},{5,1},{6,4},{7,3},{8,10},{9,13},{10,... | collective-permute-start | bytes 1572872 | tf_op jit(solution)/shard_map/ppermute | solution.py:269
  166.1 13.6 %collective-permute-start.58 = (bf16[2,8,128,128]{3,2,1,0:T(8,128)(2,1)S(1)}, bf16[2,8,128,128]{3,2,1,0:T(8,128)(2,1)S(1)}, u32[]{:S(2)}, u32[]{:S(2)}) collective-permute-start(bf16[2,8,128,128]{3,2,1,0:T(8,128)(2,1)S(1)} %add.64.refs_3_), channel_id=1, source_target_pairs={{0,2},{1,5},{2,0},{3,7},{4,6},{5,1},{6,4},{7,3},{8,10},{9,13},{10,... | collective-permute-start | bytes 1572872 | tf_op jit(solution)/shard_map/ppermute | solution.py:269
  171.3 10.3 %collective-permute-start.57 = (bf16[1,8,128,128]{3,2,1,0:T(8,128)(2,1)S(1)}, bf16[1,8,128,128]{3,2,1,0:T(8,128)(2,1)S(1)}, u32[]{:S(2)}, u32[]{:S(2)}) collective-permute-start(bf16[1,8,128,128]{3,2,1,0:T(8,128)(2,1)S(1)} %add.65.refs_3_), channel_id=1, source_target_pairs={{0,4},{1,3},{2,6},{3,1},{4,0},{5,7},{6,2},{7,5},{8,12},{9,11},{10,... | collective-permute-start | bytes 786440 | tf_op jit(solution)/shard_map/ppermute | solution.py:269
  183.1 8.8 %collective-permute-start.60 = (bf16[8,32,128]{2,1,0:T(8,128)(2,1)S(1)}, bf16[8,32,128]{2,1,0:T(8,128)(2,1)S(1)}, u32[]{:S(2)}, u32[]{:S(2)}) collective-permute-start(bf16[8,32,128]{2,1,0:T(8,128)(2,1)S(1)} %get-tuple-element.128), channel_id=1, source_target_pairs={{0,16},{8,24},{16,0},{24,8},{1,17},{9,25},{17,1},{25,9},{2,18},{10... | collective-permute-start | bytes 196616 | tf_op jit(solution)/shard_map/ppermute | solution.py:272
  186.4 11.6 %collective-permute-start.66 = (bf16[8,32,128]{2,1,0:T(8,128)(2,1)S(1)}, bf16[8,32,128]{2,1,0:T(8,128)(2,1)S(1)}, u32[]{:S(2)}, u32[]{:S(2)}) collective-permute-start(bf16[8,32,128]{2,1,0:T(8,128)(2,1)S(1)} %get-tuple-element.135), channel_id=1, source_target_pairs={{0,8},{8,0},{16,24},{24,16},{1,9},{9,1},{17,25},{25,17},{2,10},{10... | collective-permute-start | bytes 196616 | tf_op jit(solution)/shard_map/ppermute | solution.py:272
  187.5 12.8 %collective-permute-start.67 = (bf16[8,32,128]{2,1,0:T(8,128)(2,1)S(1)}, bf16[8,32,128]{2,1,0:T(8,128)(2,1)S(1)}, u32[]{:S(2)}, u32[]{:S(2)}) collective-permute-start(bf16[8,32,128]{2,1,0:T(8,128)(2,1)S(1)} %get-tuple-element.136), channel_id=1, source_target_pairs={{0,16},{8,24},{16,0},{24,8},{1,17},{9,25},{17,1},{25,9},{2,18},{10... | collective-permute-start | bytes 196616 | tf_op jit(solution)/shard_map/ppermute | solution.py:272
  189.2 11.1 %collective-permute-start.68 = (bf16[8,32,128]{2,1,0:T(8,128)(2,1)S(1)}, bf16[8,32,128]{2,1,0:T(8,128)(2,1)S(1)}, u32[]{:S(2)}, u32[]{:S(2)}) collective-permute-start(bf16[8,32,128]{2,1,0:T(8,128)(2,1)S(1)} %get-tuple-element.137), channel_id=1, source_target_pairs={{0,24},{8,16},{16,8},{24,0},{1,25},{9,17},{17,9},{25,1},{2,26},{10... | collective-permute-start | bytes 196616 | tf_op jit(solution)/shard_map/ppermute | solution.py:272
  193.0 10.6 %collective-permute-start.63 = (bf16[8,32,128]{2,1,0:T(8,128)(2,1)S(1)}, bf16[8,32,128]{2,1,0:T(8,128)(2,1)S(1)}, u32[]{:S(2)}, u32[]{:S(2)}) collective-permute-start(bf16[8,32,128]{2,1,0:T(8,128)(2,1)S(1)} %get-tuple-element.132), channel_id=1, source_target_pairs={{0,8},{8,0},{16,24},{24,16},{1,9},{9,1},{17,25},{25,17},{2,10},{10... | collective-permute-start | bytes 196616 | tf_op jit(solution)/shard_map/ppermute | solution.py:272
  (53 other events, 311.4 us)

commit v2 on v1

--- a/solution.py
+++ b/solution.py
@@ -121,13 +121,14 @@
     out_ref = refs[-1]
     lanes = lane_index(v_ref.shape[1:])
     place = (lanes % 64) // (64 // chunks)
+    signs = jnp.where((lanes < 64) == (sign > 0), -1.0, 1.0).astype(BF16)
+    masks = [jnp.where(place == a, 1.0, 0.0).astype(BF16) for a in range(chunks)]
+    masks = [(mask, mask * signs) for mask in masks]
 
     def frequency(b):
-        value = v_ref[b].astype(F32)
-        turned = pltpu.roll(value, 64, 1)
-        turned = jnp.where((lanes < 64) == (sign > 0), -turned, turned)
-        weights = [jnp.where(place == a, x, 0.0) for a in range(chunks) for x in (value, turned)]
-        weights = jnp.concatenate(weights, axis=0).astype(BF16)
+        value = v_ref[b]
+        turned = pltpu.roll(value.astype(F32), 64, 1).astype(BF16)
+        weights = jnp.concatenate([x * m for pair in masks for x, m in zip((value, turned), pair)], axis=0)
         left = []
         for pos in range(out_ref.shape[0]):
             at = places_ref[pos]

time: 212 us -> 212 us (level)
  transfers between devices with their start and end apart: 72 -> 72, of which waited for: 24 -> 22; matrix products, arithmetic and copies ran while one was open for 0% -> 0% of each run, Pallas kernels for 19% -> 19%
where the time goes in v2:
time: 212 us
  starting transfers between devices  102 us (48%)
  waiting for transfers between devices  53.5 us (25%)
  Pallas kernels  47 us (22%)
  local copies, waits for them, and re-layouts  8.03 us (4%)
    ppermute x48, starting transfers between devices, to_group(): return lax.ppermute(value, 'freq', [(z, z ^ k) for z in range(self.n_f)])  77.1 us
    ppermute x16, waiting for transfers between devices, to_chip(): return lax.ppermute(value, 'src', pairs)  44.7 us
    pallas_call x16, Pallas kernels, terms(): pl.pallas_call(functools.partial(terms_kernel, self.chunks, sign), out_sh...  29.9 us
    ppermute x16, starting transfers between devices, to_chip(): return lax.ppermute(value, 'src', pairs)  22.2 us
    pallas_call x8, Pallas kernels, window(): pl.pallas_call(functools.partial(window_kernel, self.chunks, self.n_f, mi...  8.68 us
    unnamed x26, local copies, waits for them, and re-layouts  8.03 us
    ppermute x48, waiting for transfers between devices, to_group(): return lax.ppermute(value, 'freq', [(z, z ^ k) for z in range(self.n_f)])  7.85 us
  transfers between devices with their start and end apart: 72, of which 22 were waited for; matrix products, arithmetic and copies ran while one was open for 0% of the time, Pallas kernels for 19%

profile of v2, /device:TPU:0, one launch (start us, length us, event | category | flops | bytes accessed | tf_op | source)
XLA Modules:
  0.0 211.5 jit_solution(10353746392870019203)
XLA Ops:
  3.0 3.4 %copy-done.2 = bf16[2,16,1024,128]{3,2,1,0:T(8,128)(2,1)S(1)} copy-done((bf16[2,16,1024,128]{3,2,1,0:T(8,128)(2,1)S(1)}, bf16[2,16,1024,128]{3,2,1,0:T(8,128)(2,1)}, u32[]{:S(2)}) %copy-start.2) | copy-done | bytes 8388632
  13.5 2.6 %collective-permute-start.2 = (bf16[2,8,128,128]{3,2,1,0:T(8,128)(2,1)}, bf16[2,8,128,128]{3,2,1,0:T(8,128)(2,1)S(1)}, u32[]{:S(2)}, u32[]{:S(2)}) collective-permute-start(bf16[2,8,128,128]{3,2,1,0:T(8,128)(2,1)} %copy-done.4), channel_id=1, source_target_pairs={{0,2},{1,5},{2,0},{3,7},{4,6},{5,1},{6,4},{7,3},{8,10},{9,13},{10,... | collective-permute-start | bytes 1572872 | tf_op jit(solution)/shard_map/ppermute | solution.py:270
  16.1 3.4 %copy-done.3 = bf16[2,16,1024,128]{3,2,1,0:T(8,128)(2,1)S(1)} copy-done((bf16[2,16,1024,128]{3,2,1,0:T(8,128)(2,1)S(1)}, bf16[2,16,1024,128]{3,2,1,0:T(8,128)(2,1)}, u32[]{:S(2)}) %copy-start.3) | copy-done | bytes 8388632
  23.6 2.1 %collective-permute-start.3 = (bf16[1,8,128,128]{3,2,1,0:T(8,128)(2,1)S(1)}, bf16[1,8,128,128]{3,2,1,0:T(8,128)(2,1)S(1)}, u32[]{:S(2)}, u32[]{:S(2)}) collective-permute-start(bf16[1,8,128,128]{3,2,1,0:T(8,128)(2,1)S(1)} %add.53.refs_3_), channel_id=1, source_target_pairs={{0,4},{1,3},{2,6},{3,1},{4,0},{5,7},{6,2},{7,5},{8,12},{9,11},{10,... | collective-permute-start | bytes 786440 | tf_op jit(solution)/shard_map/ppermute | solution.py:270
  25.7 7.9 %collective-permute-done.4.refs_2_ = bf16[2,8,128,128]{3,2,1,0:T(8,128)(2,1)S(1)} collective-permute-done((bf16[2,8,128,128]{3,2,1,0:T(8,128)(2,1)S(1)}, bf16[2,8,128,128]{3,2,1,0:T(8,128)(2,1)S(1)}, u32[]{:S(2)}, u32[]{:S(2)}) %collective-permute-start.4) | collective-permute-done | bytes 524320 | tf_op jit(solution)/shard_map/ppermute | solution.py:270
  37.4 2.6 %collective-permute-start.6 = (bf16[8,32,128]{2,1,0:T(8,128)(2,1)S(1)}, bf16[8,32,128]{2,1,0:T(8,128)(2,1)S(1)}, u32[]{:S(2)}, u32[]{:S(2)}) collective-permute-start(bf16[8,32,128]{2,1,0:T(8,128)(2,1)S(1)} %get-tuple-element.77), channel_id=1, source_target_pairs={{0,16},{8,24},{16,0},{24,8},{1,17},{9,25},{17,1},{25,9},{2,18},{10... | collective-permute-start | bytes 196616 | tf_op jit(solution)/shard_map/ppermute | solution.py:273
  41.9 2.7 %collective-permute-start.13 = (bf16[8,32,128]{2,1,0:T(8,128)(2,1)S(1)}, bf16[8,32,128]{2,1,0:T(8,128)(2,1)S(1)}, u32[]{:S(2)}, u32[]{:S(2)}) collective-permute-start(bf16[8,32,128]{2,1,0:T(8,128)(2,1)S(1)} %get-tuple-element.86), channel_id=1, source_target_pairs={{0,16},{8,24},{16,0},{24,8},{1,17},{9,25},{17,1},{25,9},{2,18},{10... | collective-permute-start | bytes 196616 | tf_op jit(solution)/shard_map/ppermute | solution.py:273
  47.2 2.3 %collective-permute-start.9 = (bf16[8,32,128]{2,1,0:T(8,128)(2,1)S(1)}, bf16[8,32,128]{2,1,0:T(8,128)(2,1)S(1)}, u32[]{:S(2)}, u32[]{:S(2)}) collective-permute-start(bf16[8,32,128]{2,1,0:T(8,128)(2,1)S(1)} %get-tuple-element.81), channel_id=1, source_target_pairs={{0,8},{8,0},{16,24},{24,16},{1,9},{9,1},{17,25},{25,17},{2,10},{10... | collective-permute-start | bytes 196616 | tf_op jit(solution)/shard_map/ppermute | solution.py:273
  61.9 2.0 terms.22.refs_2_
  69.3 4.1 %collective-permute-done.19.refs_2_ = bf16[2,8,128,128]{3,2,1,0:T(8,128)(2,1)S(1)} collective-permute-done((bf16[2,8,128,128]{3,2,1,0:T(8,128)(2,1)S(1)}, bf16[2,8,128,128]{3,2,1,0:T(8,128)(2,1)S(1)}, u32[]{:S(2)}, u32[]{:S(2)}) %collective-permute-start.19) | collective-permute-done | bytes 524320 | tf_op jit(solution)/shard_map/ppermute | solution.py:270
  73.5 2.0 collective-permute-start.21
  75.6 6.3 %collective-permute-done.22.refs_2_ = bf16[2,8,128,128]{3,2,1,0:T(8,128)(2,1)S(1)} collective-permute-done((bf16[2,8,128,128]{3,2,1,0:T(8,128)(2,1)S(1)}, bf16[2,8,128,128]{3,2,1,0:T(8,128)(2,1)S(1)}, u32[]{:S(2)}, u32[]{:S(2)}) %collective-permute-start.22) | collective-permute-done | bytes 524320 | tf_op jit(solution)/shard_map/ppermute | solution.py:270
  82.0 2.0 collective-permute-start.26
  86.6 2.0 collective-permute-start.25
  95.1 4.8 %collective-permute-start.27 = (bf16[8,32,128]{2,1,0:T(8,128)(2,1)S(1)}, bf16[8,32,128]{2,1,0:T(8,128)(2,1)S(1)}, u32[]{:S(2)}, u32[]{:S(2)}) collective-permute-start(bf16[8,32,128]{2,1,0:T(8,128)(2,1)S(1)} %get-tuple-element.99), channel_id=1, source_target_pairs={{0,8},{8,0},{16,24},{24,16},{1,9},{9,1},{17,25},{25,17},{2,10},{10... | collective-permute-start | bytes 196616 | tf_op jit(solution)/shard_map/ppermute | solution.py:273
  99.8 2.4 %collective-permute-start.29 = (bf16[8,32,128]{2,1,0:T(8,128)(2,1)S(1)}, bf16[8,32,128]{2,1,0:T(8,128)(2,1)S(1)}, u32[]{:S(2)}, u32[]{:S(2)}) collective-permute-start(bf16[8,32,128]{2,1,0:T(8,128)(2,1)S(1)} %get-tuple-element.101), channel_id=1, source_target_pairs={{0,24},{8,16},{16,8},{24,0},{1,25},{9,17},{17,9},{25,1},{2,26},{10... | collective-permute-start | bytes 196616 | tf_op jit(solution)/shard_map/ppermute | solution.py:273
  105.4 2.4 %collective-permute-start.36 = (bf16[8,32,128]{2,1,0:T(8,128)(2,1)S(1)}, bf16[8,32,128]{2,1,0:T(8,128)(2,1)S(1)}, u32[]{:S(2)}, u32[]{:S(2)}) collective-permute-start(bf16[8,32,128]{2,1,0:T(8,128)(2,1)S(1)} %get-tuple-element.108), channel_id=1, source_target_pairs={{0,24},{8,16},{16,8},{24,0},{1,25},{9,17},{17,9},{25,1},{2,26},{10... | collective-permute-start | bytes 196616 | tf_op jit(solution)/shard_map/ppermute | solution.py:273
  116.6 2.0 collective-permute-start.40
  118.6 5.1 %collective-permute-done.37.refs_2_ = bf16[2,8,128,128]{3,2,1,0:T(8,128)(2,1)S(1)} collective-permute-done((bf16[2,8,128,128]{3,2,1,0:T(8,128)(2,1)S(1)}, bf16[2,8,128,128]{3,2,1,0:T(8,128)(2,1)S(1)}, u32[]{:S(2)}, u32[]{:S(2)}) %collective-permute-start.37) | collective-permute-done | bytes 524320 | tf_op jit(solution)/shard_map/ppermute | solution.py:270
  123.9 8.2 %collective-permute-done.40.refs_2_ = bf16[2,8,128,128]{3,2,1,0:T(8,128)(2,1)S(1)} collective-permute-done((bf16[2,8,128,128]{3,2,1,0:T(8,128)(2,1)S(1)}, bf16[2,8,128,128]{3,2,1,0:T(8,128)(2,1)S(1)}, u32[]{:S(2)}, u32[]{:S(2)}) %collective-permute-start.40) | collective-permute-done | bytes 524320 | tf_op jit(solution)/shard_map/ppermute | solution.py:270
  134.7 2.3 %collective-permute-start.43 = (bf16[8,32,128]{2,1,0:T(8,128)(2,1)S(1)}, bf16[8,32,128]{2,1,0:T(8,128)(2,1)S(1)}, u32[]{:S(2)}, u32[]{:S(2)}) collective-permute-start(bf16[8,32,128]{2,1,0:T(8,128)(2,1)S(1)} %get-tuple-element.113), channel_id=1, source_target_pairs={{0,24},{8,16},{16,8},{24,0},{1,25},{9,17},{17,9},{25,1},{2,26},{10... | collective-permute-start | bytes 196616 | tf_op jit(solution)/shard_map/ppermute | solution.py:273
  141.0 2.3 %collective-permute-start.50 = (bf16[8,32,128]{2,1,0:T(8,128)(2,1)S(1)}, bf16[8,32,128]{2,1,0:T(8,128)(2,1)S(1)}, u32[]{:S(2)}, u32[]{:S(2)}) collective-permute-start(bf16[8,32,128]{2,1,0:T(8,128)(2,1)S(1)} %get-tuple-element.121), channel_id=1, source_target_pairs={{0,24},{8,16},{16,8},{24,0},{1,25},{9,17},{17,9},{25,1},{2,26},{10... | collective-permute-start | bytes 196616 | tf_op jit(solution)/shard_map/ppermute | solution.py:273
  146.6 2.3 %collective-permute-start.47 = (bf16[8,32,128]{2,1,0:T(8,128)(2,1)S(1)}, bf16[8,32,128]{2,1,0:T(8,128)(2,1)S(1)}, u32[]{:S(2)}, u32[]{:S(2)}) collective-permute-start(bf16[8,32,128]{2,1,0:T(8,128)(2,1)S(1)} %get-tuple-element.118), channel_id=1, source_target_pairs={{0,24},{8,16},{16,8},{24,0},{1,25},{9,17},{17,9},{25,1},{2,26},{10... | collective-permute-start | bytes 196616 | tf_op jit(solution)/shard_map/ppermute | solution.py:273
  152.1 2.3 %collective-permute-start.53 = (bf16[8,32,128]{2,1,0:T(8,128)(2,1)S(1)}, bf16[8,32,128]{2,1,0:T(8,128)(2,1)S(1)}, u32[]{:S(2)}, u32[]{:S(2)}) collective-permute-start(bf16[8,32,128]{2,1,0:T(8,128)(2,1)S(1)} %get-tuple-element.125), channel_id=1, source_target_pairs={{0,24},{8,16},{16,8},{24,0},{1,25},{9,17},{17,9},{25,1},{2,26},{10... | collective-permute-start | bytes 196616 | tf_op jit(solution)/shard_map/ppermute | solution.py:273
  161.0 3.1 %collective-permute-start.55 = (bf16[2,8,128,128]{3,2,1,0:T(8,128)(2,1)S(1)}, bf16[2,8,128,128]{3,2,1,0:T(8,128)(2,1)S(1)}, u32[]{:S(2)}, u32[]{:S(2)}) collective-permute-start(bf16[2,8,128,128]{3,2,1,0:T(8,128)(2,1)S(1)} %add.63.refs_0_), channel_id=1, source_target_pairs={{0,2},{1,5},{2,0},{3,7},{4,6},{5,1},{6,4},{7,3},{8,10},{9,13},{10,... | collective-permute-start | bytes 1572872 | tf_op jit(solution)/shard_map/ppermute | solution.py:270
  168.3 3.0 %collective-permute-done.55.refs_2_ = bf16[2,8,128,128]{3,2,1,0:T(8,128)(2,1)S(1)} collective-permute-done((bf16[2,8,128,128]{3,2,1,0:T(8,128)(2,1)S(1)}, bf16[2,8,128,128]{3,2,1,0:T(8,128)(2,1)S(1)}, u32[]{:S(2)}, u32[]{:S(2)}) %collective-permute-start.55) | collective-permute-done | bytes 524320 | tf_op jit(solution)/shard_map/ppermute | solution.py:270
  173.3 6.5 %collective-permute-done.58.refs_2_ = bf16[2,8,128,128]{3,2,1,0:T(8,128)(2,1)S(1)} collective-permute-done((bf16[2,8,128,128]{3,2,1,0:T(8,128)(2,1)S(1)}, bf16[2,8,128,128]{3,2,1,0:T(8,128)(2,1)S(1)}, u32[]{:S(2)}, u32[]{:S(2)}) %collective-permute-start.58) | collective-permute-done | bytes 524320 | tf_op jit(solution)/shard_map/ppermute | solution.py:270
  184.0 2.3 %collective-permute-start.61 = (bf16[8,32,128]{2,1,0:T(8,128)(2,1)S(1)}, bf16[8,32,128]{2,1,0:T(8,128)(2,1)S(1)}, u32[]{:S(2)}, u32[]{:S(2)}) collective-permute-start(bf16[8,32,128]{2,1,0:T(8,128)(2,1)S(1)} %get-tuple-element.129), channel_id=1, source_target_pairs={{0,24},{8,16},{16,8},{24,0},{1,25},{9,17},{17,9},{25,1},{2,26},{10... | collective-permute-start | bytes 196616 | tf_op jit(solution)/shard_map/ppermute | solution.py:273
  193.0 4.8 %collective-permute-start.63 = (bf16[8,32,128]{2,1,0:T(8,128)(2,1)S(1)}, bf16[8,32,128]{2,1,0:T(8,128)(2,1)S(1)}, u32[]{:S(2)}, u32[]{:S(2)}) collective-permute-start(bf16[8,32,128]{2,1,0:T(8,128)(2,1)S(1)} %get-tuple-element.132), channel_id=1, source_target_pairs={{0,8},{8,0},{16,24},{24,16},{1,9},{9,1},{17,25},{25,17},{2,10},{10... | collective-permute-start | bytes 196616 | tf_op jit(solution)/shard_map/ppermute | solution.py:273
  198.1 2.2 %collective-permute-start.65 = (bf16[8,32,128]{2,1,0:T(8,128)(2,1)S(1)}, bf16[8,32,128]{2,1,0:T(8,128)(2,1)S(1)}, u32[]{:S(2)}, u32[]{:S(2)}) collective-permute-start(bf16[8,32,128]{2,1,0:T(8,128)(2,1)S(1)} %get-tuple-element.134), channel_id=1, source_target_pairs={{0,24},{8,16},{16,8},{24,0},{1,25},{9,17},{17,9},{25,1},{2,26},{10... | collective-permute-start | bytes 196616 | tf_op jit(solution)/shard_map/ppermute | solution.py:273
  203.6 2.2 %collective-permute-start.71 = (bf16[8,32,128]{2,1,0:T(8,128)(2,1)S(1)}, bf16[8,32,128]{2,1,0:T(8,128)(2,1)S(1)}, u32[]{:S(2)}, u32[]{:S(2)}) collective-permute-start(bf16[8,32,128]{2,1,0:T(8,128)(2,1)S(1)} %get-tuple-element.141), channel_id=1, source_target_pairs={{0,24},{8,16},{16,8},{24,0},{1,25},{9,17},{17,9},{25,1},{2,26},{10... | collective-permute-start | bytes 196616 | tf_op jit(solution)/shard_map/ppermute | solution.py:273
  206.1 2.3 %collective-permute-done.70.refs_2_ = bf16[8,32,128]{2,1,0:T(8,128)(2,1)S(1)} collective-permute-done((bf16[8,32,128]{2,1,0:T(8,128)(2,1)S(1)}, bf16[8,32,128]{2,1,0:T(8,128)(2,1)S(1)}, u32[]{:S(2)}, u32[]{:S(2)}) %collective-permute-start.70) | collective-permute-done | bytes 65568 | tf_op jit(solution)/shard_map/ppermute | solution.py:273
  (201 shorter events, 104.4 us)
Async XLA Ops:
  13.5 10.0 %collective-permute-start.2 = (bf16[2,8,128,128]{3,2,1,0:T(8,128)(2,1)}, bf16[2,8,128,128]{3,2,1,0:T(8,128)(2,1)S(1)}, u32[]{:S(2)}, u32[]{:S(2)}) collective-permute-start(bf16[2,8,128,128]{3,2,1,0:T(8,128)(2,1)} %copy-done.4), channel_id=1, source_target_pairs={{0,2},{1,5},{2,0},{3,7},{4,6},{5,1},{6,4},{7,3},{8,10},{9,13},{10,... | collective-permute-start | bytes 1572872 | tf_op jit(solution)/shard_map/ppermute | solution.py:270
  21.5 12.1 %collective-permute-start.4 = (bf16[2,8,128,128]{3,2,1,0:T(8,128)(2,1)S(1)}, bf16[2,8,128,128]{3,2,1,0:T(8,128)(2,1)S(1)}, u32[]{:S(2)}, u32[]{:S(2)}) collective-permute-start(bf16[2,8,128,128]{3,2,1,0:T(8,128)(2,1)S(1)} %add.52.refs_0_), channel_id=1, source_target_pairs={{0,2},{1,5},{2,0},{3,7},{4,6},{5,1},{6,4},{7,3},{8,10},{9,13},{10,... | collective-permute-start | bytes 1572872 | tf_op jit(solution)/shard_map/ppermute | solution.py:270
  23.6 11.8 %collective-permute-start.3 = (bf16[1,8,128,128]{3,2,1,0:T(8,128)(2,1)S(1)}, bf16[1,8,128,128]{3,2,1,0:T(8,128)(2,1)S(1)}, u32[]{:S(2)}, u32[]{:S(2)}) collective-permute-start(bf16[1,8,128,128]{3,2,1,0:T(8,128)(2,1)S(1)} %add.53.refs_3_), channel_id=1, source_target_pairs={{0,4},{1,3},{2,6},{3,1},{4,0},{5,7},{6,2},{7,5},{8,12},{9,11},{10,... | collective-permute-start | bytes 786440 | tf_op jit(solution)/shard_map/ppermute | solution.py:270
  35.5 9.1 %collective-permute-start.5 = (bf16[8,32,128]{2,1,0:T(8,128)(2,1)S(1)}, bf16[8,32,128]{2,1,0:T(8,128)(2,1)S(1)}, u32[]{:S(2)}, u32[]{:S(2)}) collective-permute-start(bf16[8,32,128]{2,1,0:T(8,128)(2,1)S(1)} %get-tuple-element.76), channel_id=1, source_target_pairs={{0,8},{8,0},{16,24},{24,16},{1,9},{9,1},{17,25},{25,17},{2,10},{10... | collective-permute-start | bytes 196616 | tf_op jit(solution)/shard_map/ppermute | solution.py:273
  40.2 9.9 %collective-permute-start.12 = (bf16[8,32,128]{2,1,0:T(8,128)(2,1)S(1)}, bf16[8,32,128]{2,1,0:T(8,128)(2,1)S(1)}, u32[]{:S(2)}, u32[]{:S(2)}) collective-permute-start(bf16[8,32,128]{2,1,0:T(8,128)(2,1)S(1)} %get-tuple-element.85), channel_id=1, source_target_pairs={{0,8},{8,0},{16,24},{24,16},{1,9},{9,1},{17,25},{25,17},{2,10},{10... | collective-permute-start | bytes 196616 | tf_op jit(solution)/shard_map/ppermute | solution.py:273
  41.9 10.1 %collective-permute-start.13 = (bf16[8,32,128]{2,1,0:T(8,128)(2,1)S(1)}, bf16[8,32,128]{2,1,0:T(8,128)(2,1)S(1)}, u32[]{:S(2)}, u32[]{:S(2)}) collective-permute-start(bf16[8,32,128]{2,1,0:T(8,128)(2,1)S(1)} %get-tuple-element.86), channel_id=1, source_target_pairs={{0,16},{8,24},{16,0},{24,8},{1,17},{9,25},{17,1},{25,9},{2,18},{10... | collective-permute-start | bytes 196616 | tf_op jit(solution)/shard_map/ppermute | solution.py:273
  47.2 8.5 %collective-permute-start.9 = (bf16[8,32,128]{2,1,0:T(8,128)(2,1)S(1)}, bf16[8,32,128]{2,1,0:T(8,128)(2,1)S(1)}, u32[]{:S(2)}, u32[]{:S(2)}) collective-permute-start(bf16[8,32,128]{2,1,0:T(8,128)(2,1)S(1)} %get-tuple-element.81), channel_id=1, source_target_pairs={{0,8},{8,0},{16,24},{24,16},{1,9},{9,1},{17,25},{25,17},{2,10},{10... | collective-permute-start | bytes 196616 | tf_op jit(solution)/shard_map/ppermute | solution.py:273
  64.2 9.2 %collective-permute-start.19 = (bf16[2,8,128,128]{3,2,1,0:T(8,128)(2,1)S(1)}, bf16[2,8,128,128]{3,2,1,0:T(8,128)(2,1)S(1)}, u32[]{:S(2)}, u32[]{:S(2)}) collective-permute-start(bf16[2,8,128,128]{3,2,1,0:T(8,128)(2,1)S(1)} %add.55.refs_0_), channel_id=1, source_target_pairs={{0,2},{1,5},{2,0},{3,7},{4,6},{5,1},{6,4},{7,3},{8,10},{9,13},{10,... | collective-permute-start | bytes 1572872 | tf_op jit(solution)/shard_map/ppermute | solution.py:270
  66.8 15.1 %collective-permute-start.22 = (bf16[2,8,128,128]{3,2,1,0:T(8,128)(2,1)S(1)}, bf16[2,8,128,128]{3,2,1,0:T(8,128)(2,1)S(1)}, u32[]{:S(2)}, u32[]{:S(2)}) collective-permute-start(bf16[2,8,128,128]{3,2,1,0:T(8,128)(2,1)S(1)} %add.56.refs_0_), channel_id=1, source_target_pairs={{0,2},{1,5},{2,0},{3,7},{4,6},{5,1},{6,4},{7,3},{8,10},{9,13},{10,... | collective-permute-start | bytes 1572872 | tf_op jit(solution)/shard_map/ppermute | solution.py:270
  73.5 10.4 %collective-permute-start.21 = (bf16[1,8,128,128]{3,2,1,0:T(8,128)(2,1)S(1)}, bf16[1,8,128,128]{3,2,1,0:T(8,128)(2,1)S(1)}, u32[]{:S(2)}, u32[]{:S(2)}) collective-permute-start(bf16[1,8,128,128]{3,2,1,0:T(8,128)(2,1)S(1)} %add.57.refs_3_), channel_id=1, source_target_pairs={{0,4},{1,3},{2,6},{3,1},{4,0},{5,7},{6,2},{7,5},{8,12},{9,11},{10,... | collective-permute-start | bytes 786440 | tf_op jit(solution)/shard_map/ppermute | solution.py:270
  85.2 8.7 %collective-permute-start.24 = (bf16[8,32,128]{2,1,0:T(8,128)(2,1)S(1)}, bf16[8,32,128]{2,1,0:T(8,128)(2,1)S(1)}, u32[]{:S(2)}, u32[]{:S(2)}) collective-permute-start(bf16[8,32,128]{2,1,0:T(8,128)(2,1)S(1)} %get-tuple-element.95), channel_id=1, source_target_pairs={{0,16},{8,24},{16,0},{24,8},{1,17},{9,25},{17,1},{25,9},{2,18},{10... | collective-permute-start | bytes 196616 | tf_op jit(solution)/shard_map/ppermute | solution.py:273
  88.7 11.1 %collective-permute-start.30 = (bf16[8,32,128]{2,1,0:T(8,128)(2,1)S(1)}, bf16[8,32,128]{2,1,0:T(8,128)(2,1)S(1)}, u32[]{:S(2)}, u32[]{:S(2)}) collective-permute-start(bf16[8,32,128]{2,1,0:T(8,128)(2,1)S(1)} %get-tuple-element.102), channel_id=1, source_target_pairs={{0,8},{8,0},{16,24},{24,16},{1,9},{9,1},{17,25},{25,17},{2,10},{10... | collective-permute-start | bytes 196616 | tf_op jit(solution)/shard_map/ppermute | solution.py:273
  89.6 12.7 %collective-permute-start.31 = (bf16[8,32,128]{2,1,0:T(8,128)(2,1)S(1)}, bf16[8,32,128]{2,1,0:T(8,128)(2,1)S(1)}, u32[]{:S(2)}, u32[]{:S(2)}) collective-permute-start(bf16[8,32,128]{2,1,0:T(8,128)(2,1)S(1)} %get-tuple-element.103), channel_id=1, source_target_pairs={{0,16},{8,24},{16,0},{24,8},{1,17},{9,25},{17,1},{25,9},{2,18},{10... | collective-permute-start | bytes 196616 | tf_op jit(solution)/shard_map/ppermute | solution.py:273
  91.2 11.1 %collective-permute-start.32 = (bf16[8,32,128]{2,1,0:T(8,128)(2,1)S(1)}, bf16[8,32,128]{2,1,0:T(8,128)(2,1)S(1)}, u32[]{:S(2)}, u32[]{:S(2)}) collective-permute-start(bf16[8,32,128]{2,1,0:T(8,128)(2,1)S(1)} %get-tuple-element.104), channel_id=1, source_target_pairs={{0,24},{8,16},{16,8},{24,0},{1,25},{9,17},{17,9},{25,1},{2,26},{10... | collective-permute-start | bytes 196616 | tf_op jit(solution)/shard_map/ppermute | solution.py:273
  95.1 10.3 %collective-permute-start.27 = (bf16[8,32,128]{2,1,0:T(8,128)(2,1)S(1)}, bf16[8,32,128]{2,1,0:T(8,128)(2,1)S(1)}, u32[]{:S(2)}, u32[]{:S(2)}) collective-permute-start(bf16[8,32,128]{2,1,0:T(8,128)(2,1)S(1)} %get-tuple-element.99), channel_id=1, source_target_pairs={{0,8},{8,0},{16,24},{24,16},{1,9},{9,1},{17,25},{25,17},{2,10},{10... | collective-permute-start | bytes 196616 | tf_op jit(solution)/shard_map/ppermute | solution.py:273
  103.4 8.3 %collective-permute-start.34 = (bf16[8,32,128]{2,1,0:T(8,128)(2,1)S(1)}, bf16[8,32,128]{2,1,0:T(8,128)(2,1)S(1)}, u32[]{:S(2)}, u32[]{:S(2)}) collective-permute-start(bf16[8,32,128]{2,1,0:T(8,128)(2,1)S(1)} %get-tuple-element.106), channel_id=1, source_target_pairs={{0,8},{8,0},{16,24},{24,16},{1,9},{9,1},{17,25},{25,17},{2,10},{10... | collective-permute-start | bytes 196616 | tf_op jit(solution)/shard_map/ppermute | solution.py:273
  114.5 9.2 %collective-permute-start.37 = (bf16[2,8,128,128]{3,2,1,0:T(8,128)(2,1)S(1)}, bf16[2,8,128,128]{3,2,1,0:T(8,128)(2,1)S(1)}, u32[]{:S(2)}, u32[]{:S(2)}) collective-permute-start(bf16[2,8,128,128]{3,2,1,0:T(8,128)(2,1)S(1)} %add.59.refs_0_), channel_id=1, source_target_pairs={{0,2},{1,5},{2,0},{3,7},{4,6},{5,1},{6,4},{7,3},{8,10},{9,13},{10,... | collective-permute-start | bytes 1572872 | tf_op jit(solution)/shard_map/ppermute | solution.py:270
  116.6 15.5 %collective-permute-start.40 = (bf16[2,8,128,128]{3,2,1,0:T(8,128)(2,1)S(1)}, bf16[2,8,128,128]{3,2,1,0:T(8,128)(2,1)S(1)}, u32[]{:S(2)}, u32[]{:S(2)}) collective-permute-start(bf16[2,8,128,128]{3,2,1,0:T(8,128)(2,1)S(1)} %add.60.refs_3_), channel_id=1, source_target_pairs={{0,2},{1,5},{2,0},{3,7},{4,6},{5,1},{6,4},{7,3},{8,10},{9,13},{10,... | collective-permute-start | bytes 1572872 | tf_op jit(solution)/shard_map/ppermute | solution.py:270
  123.8 8.5 %collective-permute-start.39 = (bf16[1,8,128,128]{3,2,1,0:T(8,128)(2,1)S(1)}, bf16[1,8,128,128]{3,2,1,0:T(8,128)(2,1)S(1)}, u32[]{:S(2)}, u32[]{:S(2)}) collective-permute-start(bf16[1,8,128,128]{3,2,1,0:T(8,128)(2,1)S(1)} %add.61.refs_3_), channel_id=1, source_target_pairs={{0,4},{1,3},{2,6},{3,1},{4,0},{5,7},{6,2},{7,5},{8,12},{9,11},{10,... | collective-permute-start | bytes 786440 | tf_op jit(solution)/shard_map/ppermute | solution.py:270
  132.5 8.5 %collective-permute-start.41 = (bf16[8,32,128]{2,1,0:T(8,128)(2,1)S(1)}, bf16[8,32,128]{2,1,0:T(8,128)(2,1)S(1)}, u32[]{:S(2)}, u32[]{:S(2)}) collective-permute-start(bf16[8,32,128]{2,1,0:T(8,128)(2,1)S(1)} %get-tuple-element.111), channel_id=1, source_target_pairs={{0,8},{8,0},{16,24},{24,16},{1,9},{9,1},{17,25},{25,17},{2,10},{10... | collective-permute-start | bytes 196616 | tf_op jit(solution)/shard_map/ppermute | solution.py:273
  133.2 10.1 %collective-permute-start.42 = (bf16[8,32,128]{2,1,0:T(8,128)(2,1)S(1)}, bf16[8,32,128]{2,1,0:T(8,128)(2,1)S(1)}, u32[]{:S(2)}, u32[]{:S(2)}) collective-permute-start(bf16[8,32,128]{2,1,0:T(8,128)(2,1)S(1)} %get-tuple-element.112), channel_id=1, source_target_pairs={{0,16},{8,24},{16,0},{24,8},{1,17},{9,25},{17,1},{25,9},{2,18},{10... | collective-permute-start | bytes 196616 | tf_op jit(solution)/shard_map/ppermute | solution.py:273
  134.7 8.6 %collective-permute-start.43 = (bf16[8,32,128]{2,1,0:T(8,128)(2,1)S(1)}, bf16[8,32,128]{2,1,0:T(8,128)(2,1)S(1)}, u32[]{:S(2)}, u32[]{:S(2)}) collective-permute-start(bf16[8,32,128]{2,1,0:T(8,128)(2,1)S(1)} %get-tuple-element.113), channel_id=1, source_target_pairs={{0,24},{8,16},{16,8},{24,0},{1,25},{9,17},{17,9},{25,1},{2,26},{10... | collective-permute-start | bytes 196616 | tf_op jit(solution)/shard_map/ppermute | solution.py:273
  139.5 9.3 %collective-permute-start.49 = (bf16[8,32,128]{2,1,0:T(8,128)(2,1)S(1)}, bf16[8,32,128]{2,1,0:T(8,128)(2,1)S(1)}, u32[]{:S(2)}, u32[]{:S(2)}) collective-permute-start(bf16[8,32,128]{2,1,0:T(8,128)(2,1)S(1)} %get-tuple-element.120), channel_id=1, source_target_pairs={{0,16},{8,24},{16,0},{24,8},{1,17},{9,25},{17,1},{25,9},{2,18},{10... | collective-permute-start | bytes 196616 | tf_op jit(solution)/shard_map/ppermute | solution.py:273
  145.5 9.0 %collective-permute-start.46 = (bf16[8,32,128]{2,1,0:T(8,128)(2,1)S(1)}, bf16[8,32,128]{2,1,0:T(8,128)(2,1)S(1)}, u32[]{:S(2)}, u32[]{:S(2)}) collective-permute-start(bf16[8,32,128]{2,1,0:T(8,128)(2,1)S(1)} %get-tuple-element.117), channel_id=1, source_target_pairs={{0,16},{8,24},{16,0},{24,8},{1,17},{9,25},{17,1},{25,9},{2,18},{10... | collective-permute-start | bytes 196616 | tf_op jit(solution)/shard_map/ppermute | solution.py:273
  161.0 10.3 %collective-permute-start.55 = (bf16[2,8,128,128]{3,2,1,0:T(8,128)(2,1)S(1)}, bf16[2,8,128,128]{3,2,1,0:T(8,128)(2,1)S(1)}, u32[]{:S(2)}, u32[]{:S(2)}) collective-permute-start(bf16[2,8,128,128]{3,2,1,0:T(8,128)(2,1)S(1)} %add.63.refs_0_), channel_id=1, source_target_pairs={{0,2},{1,5},{2,0},{3,7},{4,6},{5,1},{6,4},{7,3},{8,10},{9,13},{10,... | collective-permute-start | bytes 1572872 | tf_op jit(solution)/shard_map/ppermute | solution.py:270
  166.1 13.6 %collective-permute-start.58 = (bf16[2,8,128,128]{3,2,1,0:T(8,128)(2,1)S(1)}, bf16[2,8,128,128]{3,2,1,0:T(8,128)(2,1)S(1)}, u32[]{:S(2)}, u32[]{:S(2)}) collective-permute-start(bf16[2,8,128,128]{3,2,1,0:T(8,128)(2,1)S(1)} %add.64.refs_3_), channel_id=1, source_target_pairs={{0,2},{1,5},{2,0},{3,7},{4,6},{5,1},{6,4},{7,3},{8,10},{9,13},{10,... | collective-permute-start | bytes 1572872 | tf_op jit(solution)/shard_map/ppermute | solution.py:270
  171.4 10.3 %collective-permute-start.57 = (bf16[1,8,128,128]{3,2,1,0:T(8,128)(2,1)S(1)}, bf16[1,8,128,128]{3,2,1,0:T(8,128)(2,1)S(1)}, u32[]{:S(2)}, u32[]{:S(2)}) collective-permute-start(bf16[1,8,128,128]{3,2,1,0:T(8,128)(2,1)S(1)} %add.65.refs_3_), channel_id=1, source_target_pairs={{0,4},{1,3},{2,6},{3,1},{4,0},{5,7},{6,2},{7,5},{8,12},{9,11},{10,... | collective-permute-start | bytes 786440 | tf_op jit(solution)/shard_map/ppermute | solution.py:270
  183.2 8.8 %collective-permute-start.60 = (bf16[8,32,128]{2,1,0:T(8,128)(2,1)S(1)}, bf16[8,32,128]{2,1,0:T(8,128)(2,1)S(1)}, u32[]{:S(2)}, u32[]{:S(2)}) collective-permute-start(bf16[8,32,128]{2,1,0:T(8,128)(2,1)S(1)} %get-tuple-element.128), channel_id=1, source_target_pairs={{0,16},{8,24},{16,0},{24,8},{1,17},{9,25},{17,1},{25,9},{2,18},{10... | collective-permute-start | bytes 196616 | tf_op jit(solution)/shard_map/ppermute | solution.py:273
  186.4 11.6 %collective-permute-start.66 = (bf16[8,32,128]{2,1,0:T(8,128)(2,1)S(1)}, bf16[8,32,128]{2,1,0:T(8,128)(2,1)S(1)}, u32[]{:S(2)}, u32[]{:S(2)}) collective-permute-start(bf16[8,32,128]{2,1,0:T(8,128)(2,1)S(1)} %get-tuple-element.135), channel_id=1, source_target_pairs={{0,8},{8,0},{16,24},{24,16},{1,9},{9,1},{17,25},{25,17},{2,10},{10... | collective-permute-start | bytes 196616 | tf_op jit(solution)/shard_map/ppermute | solution.py:273
  187.5 12.8 %collective-permute-start.67 = (bf16[8,32,128]{2,1,0:T(8,128)(2,1)S(1)}, bf16[8,32,128]{2,1,0:T(8,128)(2,1)S(1)}, u32[]{:S(2)}, u32[]{:S(2)}) collective-permute-start(bf16[8,32,128]{2,1,0:T(8,128)(2,1)S(1)} %get-tuple-element.136), channel_id=1, source_target_pairs={{0,16},{8,24},{16,0},{24,8},{1,17},{9,25},{17,1},{25,9},{2,18},{10... | collective-permute-start | bytes 196616 | tf_op jit(solution)/shard_map/ppermute | solution.py:273
  189.2 11.1 %collective-permute-start.68 = (bf16[8,32,128]{2,1,0:T(8,128)(2,1)S(1)}, bf16[8,32,128]{2,1,0:T(8,128)(2,1)S(1)}, u32[]{:S(2)}, u32[]{:S(2)}) collective-permute-start(bf16[8,32,128]{2,1,0:T(8,128)(2,1)S(1)} %get-tuple-element.137), channel_id=1, source_target_pairs={{0,24},{8,16},{16,8},{24,0},{1,25},{9,17},{17,9},{25,1},{2,26},{10... | collective-permute-start | bytes 196616 | tf_op jit(solution)/shard_map/ppermute | solution.py:273
  193.0 10.6 %collective-permute-start.63 = (bf16[8,32,128]{2,1,0:T(8,128)(2,1)S(1)}, bf16[8,32,128]{2,1,0:T(8,128)(2,1)S(1)}, u32[]{:S(2)}, u32[]{:S(2)}) collective-permute-start(bf16[8,32,128]{2,1,0:T(8,128)(2,1)S(1)} %get-tuple-element.132), channel_id=1, source_target_pairs={{0,8},{8,0},{16,24},{24,16},{1,9},{9,1},{17,25},{25,17},{2,10},{10... | collective-permute-start | bytes 196616 | tf_op jit(solution)/shard_map/ppermute | solution.py:273
  (53 other events, 311.0 us)
